TPU v7x, 512 devices: a whole 4x4x16 slice. The times are simulated.
512 devices in a mesh: row: 16 (over x_hi, y, core), col: 32 (over z, x_lo).
Axes of the slice: x: 4 (x_hi: 2, x_lo: 2; x = x_hi * 2 + x_lo), y: 4, z: 16, core: 2. Of those that a mesh axis runs over, the one named last changes fastest.
Arguments:
- embeddings: bfloat16 [32768, 256], P(('row', 'col')), may hold values from -1 to 1, as said below
- prior_scores: bfloat16 [32768, 128], P(('row', 'col')), may hold values from -6 to 6
- seed_labels: int32 [32768], P(('row', 'col')), may hold values from 0 to 255
- tile_pattern: int32 [32, 32], P('row', 'col'), may hold values from 0 to 1, as said below
Outputs:
- label_scores: float32 [32768, 128], P(('row', 'col'))
Inputs may be any that keep to these rules, and one draw needn't show every extreme that they name: `embeddings`: each row has length one up to bfloat16 rounding. `tile_pattern`: symmetric; every tile on the diagonal is kept; counts of kept tiles differ from row block to row block. `seed_labels`: a value of 128 or more marks a node without a seed.
All inputs are finite; a program needn't handle non-finite values.
Results may differ from a plain program's by a relative error of at most 0.006.
Values may be sent and summed in bfloat16 or wider, within the bound.
No kernel may reach another device: no remote copies, remote signals or barrier semaphores. Data moves between devices by JAX's collectives and lax.ppermute only.
A program may use at most 64 MiB of HBM per device.

v0:
```python
import jax
import jax.numpy as jnp
from jax import lax
from jax.sharding import PartitionSpec as P

TILE = 1024
ITERS = 2


KERNEL_SPREAD = 0.05
PROPAGATE_WEIGHT = 0.9
SEED_WEIGHT = 0.1


def broadcast(shard, axis, root):
    mine = lax.axis_index(axis) == root
    return lax.psum(jnp.where(mine, shard, jnp.zeros_like(shard)), axis)


def add_block(totals, value, where):
    current = lax.dynamic_index_in_dim(totals, where, 0, False)
    return lax.dynamic_update_index_in_dim(totals, current + value, where, 0)


def per_device(embeddings, prior_scores, seed_labels, tile_pattern):
    row_total = lax.axis_size("row")
    col_total = lax.axis_size("col")
    col_index = lax.axis_index("col")
    emb_panel, prior_panel = (
        lax.all_gather(embeddings, "col", axis=0, tiled=True),
        lax.all_gather(prior_scores, "col", axis=0, tiled=True),
    )
    panel_rows = emb_panel.shape[0]
    column_rows = panel_rows * row_total // col_total
    col_ratio = col_total // row_total
    offset = col_index % col_ratio * column_rows
    source = col_index // col_ratio
    emb_cols = broadcast(lax.dynamic_slice_in_dim(emb_panel, offset, column_rows, 0), "row", source)
    row_tiles, col_tiles = tile_pattern.shape
    flat_pattern = tile_pattern.reshape(-1)
    slot_order = jnp.argsort(1 - flat_pattern, stable=True)
    live_count = jnp.sum(flat_pattern)
    classes = prior_scores.shape[1]

    def locate(slot):
        index = slot_order[slot]
        return (index // col_tiles, index % col_tiles)

    def make_tile(slot):
        row_block_part, column_block_part = locate(slot)
        left_rows = lax.dynamic_slice_in_dim(emb_panel, row_block_part * TILE, TILE, 0)
        label_weights = jnp.einsum(
            "ie,je->ij", left_rows, emb_cols, preferred_element_type=jnp.float32
        )
        return (
            jnp.exp((label_weights - 1.0) / KERNEL_SPREAD).astype(jnp.bfloat16),
            row_block_part,
            column_block_part,
        )

    sums_init = jnp.zeros((row_tiles, TILE), jnp.float32)
    tile_cache = jnp.zeros((row_tiles * col_tiles, TILE, TILE), jnp.bfloat16)

    def degree_step(slot, carry):
        sums, cache_now = carry
        tile, row_block_part, column_block_part = make_tile(slot)
        sums = add_block(sums, jnp.sum(tile, axis=1, dtype=jnp.float32), row_block_part)
        cache_now = lax.dynamic_update_index_in_dim(cache_now, tile, slot, 0)
        return (sums, cache_now)

    row_sums, tile_cache = lax.fori_loop(0, live_count, degree_step, (sums_init, tile_cache))

    def fetch(slot):
        row_block_part, column_block_part = locate(slot)
        return (
            lax.dynamic_index_in_dim(tile_cache, slot, 0, False),
            row_block_part,
            column_block_part,
        )

    degree = lax.psum(row_sums.reshape(-1), "col")
    inv_degree = 1.0 / jnp.sqrt(degree)
    shard_rows = embeddings.shape[0]
    own_start = col_index * shard_rows
    classes_iota = jnp.arange(classes, dtype=jnp.int32)
    label_panel = lax.all_gather(seed_labels, "col", axis=0, tiled=True)
    seed_block_rows = (label_panel[:, None] == classes_iota[None, :]).astype(jnp.float32)
    scaled_panel = (inv_degree[:, None] * prior_panel.astype(jnp.float32)).astype(jnp.bfloat16)
    result = prior_scores.astype(jnp.float32)
    for sweep in range(ITERS):
        normalized_columns = broadcast(
            lax.dynamic_slice_in_dim(scaled_panel, offset, column_rows, 0), "row", source
        )

        def step(slot, totals):
            tile, row_block_part, column_block_part = fetch(slot)
            return add_block(
                totals,
                jnp.dot(tile, normalized_columns, preferred_element_type=jnp.float32),
                row_block_part,
            )

        totals = lax.fori_loop(
            0, live_count, step, jnp.zeros((row_tiles, TILE, classes), jnp.float32)
        )
        partial_panel = totals.reshape(panel_rows, classes)
        summed = lax.psum(partial_panel, "col")
        new_panel = PROPAGATE_WEIGHT * inv_degree[:, None] * summed + SEED_WEIGHT * seed_block_rows
        scaled_panel = (inv_degree[:, None] * new_panel).astype(jnp.bfloat16)
        result = lax.dynamic_slice_in_dim(new_panel, own_start, shard_rows, 0)
    return result


def solution(mesh):
    return jax.shard_map(
        per_device,
        mesh=mesh,
        in_specs=(
            P(("row", "col"), None),
            P(("row", "col"), None),
            P(("row", "col")),
            P("row", "col"),
        ),
        out_specs=P(("row", "col"), None),
        check_vma=False,
    )
```

profile of v0, /device:TPU:8, one launch (start us, length us, event | category | flops | bytes accessed | tf_op | source)
XLA Modules:
  0.0 1263.2 jit_solution(2732554605086666592)
XLA Ops:
  6.5 0.7 all-gather.2.cloned.1.call-update
  7.3 0.0 all-reduce.7.cloned.1.call-start
  7.3 137.9 %all-gather.2.cloned.1.call-done = bf16[2048,256]{1,0:T(8,128)(2,1)} async-done(((bf16[64,256]{1,0:T(8,128)(2,1)}), bf16[2048,256]{1,0:T(8,128)(2,1)}) %all-gather.2.cloned.1.call-update) | async-done | bytes 1048592 | tf_op jit(solution)/shard_map/all_gather | solution.py:30
  145.3 1.9 dynamic-slice_select_fusion
  147.2 0.0 all-reduce.7.cloned.1.call-update
  147.2 0.0 all-reduce.9.cloned.1.call-start
  147.3 1.4 subtract_bitcast_fusion
  148.7 0.6 sort.17
  149.3 63.7 %all_gather.10 = bf16[2048,128]{1,0:T(8,128)(2,1)S(1)} all-gather(bf16[64,128]{1,0:T(8,128)(2,1)} %param.11), channel_id=1, replica_groups=mesh['row'=16,'col'=32] {'col'}, dimensions={0}, use_global_device_ids=true | all-gather | bytes 540672 | tf_op jit(solution)/shard_map/all_gather | solution.py:31
  213.0 83.9 %all-reduce.7.cloned.1.call-done = bf16[1024,256]{1,0:T(8,128)(2,1)} async-done(((bf16[1024,256]{1,0:T(8,128)(2,1)}), bf16[1024,256]{1,0:T(8,128)(2,1)}) %all-reduce.7.cloned.1.call-update) | async-done | bytes 524304 | tf_op jit(solution)/shard_map/psum | solution.py:17
  296.9 2.5 broadcast_in_dim.38.clone
  299.4 12.1 while.38
  300.1 0.6 dynamic_slice.134
  301.3 3.3 convert_reduce_fusion.2
  304.6 2.9 copy.13
  307.5 1.5 constant_dynamic-update-slice_fusion.2
  310.8 0.1 dynamic_update_slice.35
  311.6 72.5 %psum.43 = f32[2048]{0:T(1024)S(1)} all-reduce(f32[2048]{0:T(1024)S(1)} %bitcast.80), channel_id=1, replica_groups=mesh['row'=16,'col'=32] {'col'}, use_global_device_ids=true, to_apply=%region_6.7 | all-reduce | flops 2048 | bytes 16384 | tf_op jit(solution)/shard_map/psum | solution.py:81
  384.0 0.9 fusion.31
  385.0 0.0 all-reduce.9.cloned.1.call-update
  385.0 0.0 all-reduce.11.cloned.1.call-start
  385.0 152.5 %all-reduce.9.cloned.1.call-done = bf16[1024,128]{1,0:T(8,128)(2,1)} async-done(((bf16[1024,128]{1,0:T(8,128)(2,1)}), bf16[1024,128]{1,0:T(8,128)(2,1)}) %all-reduce.9.cloned.1.call-update) | async-done | bytes 262160 | tf_op jit(solution)/shard_map/psum | solution.py:17
  537.5 0.1 broadcast.45.clone
  537.6 0.0 copy-start.3
  537.6 6.1 while.39
  538.3 0.6 dynamic_slice.137
  540.7 2.3 fusion.46
  543.7 1.0 copy-done.1
  544.7 0.0 all-reduce.11.cloned.1.call-update
  544.7 0.0 all-reduce.13.cloned.1.call-start
  544.8 1.3 dynamic-slice
  546.7 0.3 dynamic-update-slice
  547.0 25.5 %all-reduce = s32[2048]{0:T(1024)S(1)} all-reduce(s32[2048]{0:T(1024)S(1)} %dynamic-update-slice), channel_id=1, replica_groups=mesh['row'=16,'col'=32] {'col'}, use_global_device_ids=true, to_apply=%add | all-reduce | flops 2048 | bytes 16384
  572.5 0.3 fusion.28
  572.9 248.2 %all-reduce.11.cloned.1.call-done = f32[2048,128]{1,0:T(8,128)} async-done(((f32[2048,128]{1,0:T(8,128)}), f32[2048,128]{1,0:T(8,128)}) %all-reduce.11.cloned.1.call-update) | async-done | bytes 1048592 | tf_op jit(solution)/shard_map/psum | solution.py:107
  821.0 2.1 fusion.32
  823.1 0.0 all-reduce.13.cloned.1.call-update
  823.2 0.0 all-reduce.15.cloned.1.call-start
  823.2 148.2 %all-reduce.13.cloned.1.call-done = bf16[1024,128]{1,0:T(8,128)(2,1)} async-done(((bf16[1024,128]{1,0:T(8,128)(2,1)}), bf16[1024,128]{1,0:T(8,128)(2,1)}) %all-reduce.13.cloned.1.call-update) | async-done | bytes 262160 | tf_op jit(solution)/shard_map/psum | solution.py:17
  971.4 0.1 broadcast.45
  971.5 6.1 while.40
  972.2 0.6 dynamic_slice.140
  974.6 2.3 fusion.49
  977.6 1.0 copy-done
  978.6 0.0 all-reduce.15.cloned.1.call-update
  978.6 0.1 dynamic-slice.4
  978.7 276.2 %all-reduce.15.cloned.1.call-done = f32[2048,128]{1,0:T(8,128)} async-done(((f32[2048,128]{1,0:T(8,128)}), f32[2048,128]{1,0:T(8,128)}) %all-reduce.15.cloned.1.call-update) | async-done | bytes 1048592 | tf_op jit(solution)/shard_map/psum | solution.py:107
  1254.9 1.4 dynamic-slice_add_fusion.2
  (16 shorter events, 0.1 us)
Async XLA Ops:
  6.5 138.7 %all-gather.2.cloned.1.call-start = ((), (), s32[]{:S(2)}) async-start(), calls=%async_computation | async-start | bytes 1081344 | tf_op jit(solution)/shard_map/all_gather | solution.py:30
  7.3 289.7 %all-reduce.7.cloned.1.call-start = ((), (), s32[]{:S(2)}) async-start(), calls=%async_computation.1 | async-start | bytes 1048576 | tf_op jit(solution)/shard_map/psum | solution.py:17
  147.2 390.3 %all-reduce.9.cloned.1.call-start = ((), (), s32[]{:S(2)}) async-start(), calls=%async_computation.2 | async-start | bytes 524288 | tf_op jit(solution)/shard_map/psum | solution.py:17
  296.9 2.5 copy-start.2
  385.0 436.1 %all-reduce.11.cloned.1.call-start = ((), (), s32[]{:S(2)}) async-start(), calls=%async_computation.3 | async-start | bytes 2097152 | tf_op jit(solution)/shard_map/psum | solution.py:107
  537.6 9.1 copy-start.3
  543.7 1.0 copy-start.1
  544.7 426.7 %all-reduce.13.cloned.1.call-start = ((), (), s32[]{:S(2)}) async-start(), calls=%async_computation.4 | async-start | bytes 524288 | tf_op jit(solution)/shard_map/psum | solution.py:17
  823.2 431.7 %all-reduce.15.cloned.1.call-start = ((), (), s32[]{:S(2)}) async-start(), calls=%async_computation.5 | async-start | bytes 2097152 | tf_op jit(solution)/shard_map/psum | solution.py:107
  977.6 1.0 copy-start
Sparse Core Ops, SparseCore 0:
  9.4 135.7 all-gather.1
  148.2 148.7 all-reduce.6
  385.1 152.3 all-reduce.8
  544.9 276.1 all-reduce.10
  824.0 147.3 all-reduce.12
  978.7 276.0 all-reduce.14
where the time goes:
time: 1260 us
  waiting for transfers between devices  1050 us (83%)
  blocking collectives  162 us (13%)
  between operations  14.3 us (1%)
  local copies, waits for them, and re-layouts  12.6 us (1%)
    psum x2, waiting for transfers between devices, per_device(): summed = lax.psum(partial_panel, 'col')  524 us
    psum x3, waiting for transfers between devices, broadcast(): return lax.psum(jnp.where(mine, shard, jnp.zeros_like(shard)), axis)  385 us
    all_gather x1, waiting for transfers between devices, per_device(): lax.all_gather(embeddings, 'col', axis=0, tiled=True)  138 us
    psum x1, blocking collectives, per_device(): degree = lax.psum(row_sums.reshape(-1), 'col')  72.5 us
    all_gather x1, blocking collectives, per_device(): lax.all_gather(prior_scores, 'col', axis=0, tiled=True)  63.7 us
    unnamed x1, blocking collectives  25.5 us
  transfers between devices with their start and end apart: 6, of which 6 were waited for; matrix products, arithmetic and copies ran while one was open for 0% of the time, Pallas kernels for 0%

commit v1 on v0

v1 whole, which is shorter than its diff:
```python
import jax
import jax.numpy as jnp
from jax import lax
from jax.sharding import Mesh, PartitionSpec as P

KERNEL_SPREAD = 0.05
PROPAGATE_WEIGHT = 0.9
SEED_WEIGHT = 0.1

AXES = ("xh", "y", "core", "z", "xl")
SIZES = (2, 4, 2, 16, 2)
ROW = ("xh", "y", "core")
COL = ("z", "xl")
PLANE = ("xh", "y", "xl")
LANES = 128


def spread_gather(x, axes, count):
    copies = jnp.broadcast_to(x[None], (count,) + x.shape)
    return lax.all_to_all(copies, axes, 0, 0, tiled=True)


def per_device(embeddings, prior_scores, seed_labels, tile_pattern):
    bf, f32 = jnp.bfloat16, jnp.float32
    nodes, classes = prior_scores.shape
    z = lax.axis_index("z")
    z_half = z // 8
    halves = [embeddings[:, :LANES], embeddings[:, LANES:]]
    pattern = tile_pattern.astype(bf)

    flags = jnp.broadcast_to(jnp.repeat(pattern[:, 0], LANES // 2)[None, :], (8, LANES))
    panel = spread_gather(jnp.concatenate(halves + [flags], 0), PLANE, 16)
    panel = lax.all_gather(panel, "core", axis=0)
    emb_b = jnp.concatenate([panel[:, :, :nodes], panel[:, :, nodes : 2 * nodes]], 3)
    emb_b = emb_b.reshape(32 * nodes, 2 * LANES)
    flags = panel[:, :, 2 * nodes, :: LANES // 2].reshape(2, 2, 4, 2, 2)
    flags = flags[lax.axis_index("core"), lax.axis_index("xh"), lax.axis_index("y")]

    flags = jnp.broadcast_to(flags.reshape(4, 1), (4, LANES))
    flags = jnp.concatenate([flags, flags], 0)
    column = lax.all_gather(jnp.concatenate(halves + [prior_scores, flags], 0), "z", axis=0)
    emb_a = jnp.concatenate([column[:, :nodes], column[:, nodes : 2 * nodes]], 2)
    emb_a = emb_a.reshape(16 * nodes, 2 * LANES)
    prior_a = column[:, 2 * nodes : 3 * nodes].reshape(16 * nodes, classes)
    kept = column[:, 3 * nodes : 3 * nodes + 4, 0].reshape(16, 2, 2)
    kept = lax.dynamic_index_in_dim(kept, z_half, 1, False)
    kept = kept.reshape(2, 4, 2, 2).transpose(2, 0, 1, 3).reshape(16, 2)

    weights = lax.dot_general(emb_b, emb_a, (((1,), (1,)), ((), ())), preferred_element_type=f32)
    kernel = jnp.exp((weights - 1.0) / KERNEL_SPREAD)
    keep = jnp.broadcast_to(kept[:, None, :, None], (16, 2 * nodes, 2, 8 * nodes))
    kernel = jnp.where(keep.reshape(kernel.shape) > 0, kernel, 0.0).astype(bf)

    partial = jnp.sum(kernel, axis=0, dtype=f32).reshape(8, LANES)
    degree = jnp.sum(spread_gather(partial, "z", 16), axis=0).reshape(16, nodes)
    inv = 1.0 / jnp.sqrt(degree)
    inv_own = lax.dynamic_index_in_dim(inv, z, 0, False)[:, None]
    inv = inv.reshape(-1, 1)
    classes_iota = jnp.arange(classes, dtype=jnp.int32)
    seeds = SEED_WEIGHT * (seed_labels[:, None] == classes_iota[None, :]).astype(f32)

    scaled_a = (inv * prior_a.astype(f32)).astype(bf)
    part = jnp.dot(kernel, scaled_a, preferred_element_type=f32).astype(bf)
    part = lax.all_to_all(part.reshape(32, nodes, classes), ("core",) + PLANE, 0, 0, tiled=True)
    product = jnp.sum(part.astype(f32), axis=0)
    scores = PROPAGATE_WEIGHT * inv_own * product + seeds

    scaled = (inv_own * scores).astype(bf)
    scaled_b = lax.all_gather(spread_gather(scaled, PLANE, 16), "core", axis=0)
    scaled_b = scaled_b.reshape(32 * nodes, classes)
    part = lax.dot_general(kernel, scaled_b, (((0,), (0,)), ((), ())), preferred_element_type=f32)
    part = lax.all_to_all(part.astype(bf).reshape(16, nodes, classes), "z", 0, 0, tiled=True)
    product = jnp.sum(part.astype(f32), axis=0)
    return PROPAGATE_WEIGHT * inv_own * product + seeds


def solution(mesh):
    return jax.shard_map(
        per_device,
        mesh=Mesh(mesh.devices.reshape(SIZES), AXES),
        in_specs=(P(AXES, None), P(AXES, None), P(AXES), P(ROW, COL)),
        out_specs=P(AXES, None),
        check_vma=False,
    )
```

time: 1260 us -> 189 us (0.15)
  the two profiles are of different devices: /device:TPU:8 before, /device:TPU:32 now
where the time goes in v1:
time: 189 us
  blocking collectives  111 us (59%)
  waiting for transfers between devices  31.5 us (17%)
  between operations  13.5 us (7%)
  matrix products  12 us (6%)
  local copies, waits for them, and re-layouts  11.1 us (6%)
  starting transfers between devices  7.09 us (4%)
    all_to_all x3, blocking collectives, spread_gather(): return lax.all_to_all(copies, axes, 0, 0, tiled=True)  53.5 us
    all_gather x1, blocking collectives, per_device(): lax.all_gather(jnp.concatenate(halves + [prior_scores, flags], 0), 'z', a...  33.5 us
    all_to_all x1, blocking collectives, per_device(): lax.all_to_all(part.astype(bf).reshape(16, nodes, classes), 'z', 0, 0, ti...  22.3 us
    all_gather x1, waiting for transfers between devices, per_device(): panel = lax.all_gather(panel, 'core', axis=0)  20.1 us
    all_to_all x1, waiting for transfers between devices, per_device(): lax.all_to_all(part.reshape(32, nodes, classes), ('core',) + PLANE, 0, 0,...  11.5 us
    all_to_all x1, starting transfers between devices, per_device(): lax.all_to_all(part.reshape(32, nodes, classes), ('core',) + PLANE, 0, 0,...  7.09 us
    gt x4, local copies, waits for them, and re-layouts, per_device(): kernel = jnp.where(keep.reshape(kernel.shape) > 0, kernel, 0.0).astype(bf)  5.09 us
    dot_general x1, matrix products, per_device(): part = jnp.dot(kernel, scaled_a, preferred_element_type=f32).astype(bf)  4.35 us
  transfers between devices with their start and end apart: 2, of which 2 were waited for; matrix products, arithmetic and copies ran while one was open for 0% of the time, Pallas kernels for 0%

profile of v1, /device:TPU:32, one launch (start us, length us, event | category | flops | bytes accessed | tf_op | source)
XLA Modules:
  0.0 188.6 jit_solution(12010514781258542547)
XLA Ops:
  6.5 0.0 copy-start
  6.5 0.0 all-gather.5.cloned.1.call-start
  6.5 0.7 convert_bitcast_fusion
  7.2 0.1 broadcast_in_dim.50
  7.3 0.1 broadcast_in_dim.51
  7.4 0.7 fusion.10
  8.1 0.1 broadcast_in_dim.53
  8.2 19.0 %all_to_all.25 = bf16[16,136,128]{2,1,0:T(8,128)(2,1)} all-to-all(bf16[16,136,128]{2,1,0:T(8,128)(2,1)S(1)} %broadcast_in_dim.53), channel_id=1, replica_groups=mesh['xh'=2,'y'=4,'core'=2,'z'=16,'xl'=2] {'xh','y','xl'}, dimensions={0} | all-to-all | bytes 1114112 | tf_op jit(solution)/shard_map/all_to_all | solution.py:20
  27.2 0.0 all-gather.5.cloned.1.call-update
  27.2 20.1 %all-gather.5.cloned.1.call-done = bf16[32,136,128]{2,1,0:T(8,128)(2,1)} async-done(((bf16[16,136,128]{2,1,0:T(8,128)(2,1)}), bf16[32,136,128]{2,1,0:T(8,128)(2,1)}) %all-gather.5.cloned.1.call-update) | async-done | bytes 1114128 | tf_op jit(solution)/shard_map/all_gather | solution.py:33
  47.3 1.0 slice.29
  48.3 1.3 fusion.8
  49.5 0.1 copy.19
  49.6 0.1 reshape_squeeze.7
  49.7 0.1 copy.20
  49.9 0.1 broadcast_in_dim.54
  49.9 0.1 broadcast_in_dim.55
  50.0 0.0 copy-done
  50.0 0.1 concatenate.13
  50.1 33.5 %all-gather.1 = bf16[3200,128]{1,0:T(8,128)(2,1)S(1)} all-gather(bf16[200,128]{1,0:T(8,128)(2,1)S(1)} %concatenate.13), channel_id=3, replica_groups=mesh['xh'=2,'y'=4,'core'=2,'z'=16,'xl'=2] {'z'}, dimensions={0}, use_global_device_ids=true | all-gather | bytes 870400 | tf_op jit(solution)/shard_map/all_gather | solution.py:41
  83.6 0.1 fusion.9
  83.7 0.1 copy.24
  83.8 0.1 gt.21
  83.9 0.1 copy.22
  84.1 0.1 gt.23
  84.2 0.6 broadcast_in_dim.56
  84.8 1.3 copy.27
  86.1 4.8 %copy.23 = pred[2048,1024]{1,0:T(32,128)(4,1)S(1)} copy(pred[2048,1024]{0,1:T(8,128)(4,1)S(1)} %bitcast.38) | data formatting | bytes 4194304 | tf_op jit(solution)/shard_map/gt | solution.py:52
  90.8 0.1 pad_maximum_fusion
  91.0 0.1 pad_maximum_fusion.1
  91.1 4.2 %convert_reduce_fusion = (f32[1024]{0:T(1024)S(1)}, bf16[2048,1024]{1,0:T(8,128)(2,1)}) fusion(pred[2048,1024]{1,0:T(32,128)(4,1)S(1)} %copy.23, bf16[2048,256]{1,0:T(8,128)(2,1)S(1)} %bitcast.41, bf16[1024,256]{1,0:T(8,128)(2,1)S(1)} %bitcast.45), kind=kOutput, calls=%fused_computation | convolution fusion | flops 1086323712 | bytes 7868416 | tf_op jit(solution)/shard_map/dot_general | solution.py:49
  95.2 0.0 copy-start.1
  95.2 21.9 %all_to_all.26 = f32[16,8,128]{2,1,0:T(8,128)S(1)} all-to-all(f32[16,8,128]{2,1,0:T(8,128)S(1)} %broadcast_in_dim.59), channel_id=1, replica_groups=mesh['xh'=2,'y'=4,'core'=2,'z'=16,'xl'=2] {'z'}, dimensions={0} | all-to-all | bytes 131072 | tf_op jit(solution)/shard_map/all_to_all | solution.py:20
  117.2 4.3 %convolution_convert_fusion = bf16[2048,128]{1,0:T(8,128)(2,1)} fusion(bf16[2048,1024]{1,0:T(8,128)(2,1)} %get-tuple-element.17, bf16[1024,128]{1,0:T(8,128)(2,1)S(1)} %bitcast.47, f32[1024]{0:T(1024)S(1)} %get-tuple-element.15), kind=kOutput, calls=%fused_computation.3 | convolution fusion | flops 537526272 | bytes 4984832 | tf_op jit(solution)/shard_map/dot_general | solution.py:63
  121.6 7.1 %all-to-all-start.2 = ((bf16[32,64,128]{2,1,0:T(8,128)(2,1)}), bf16[32,64,128]{2,1,0:T(8,128)(2,1)S(1)}, u32[]{:S(2)}, u32[]{:S(2)}) async-start(bf16[32,64,128]{2,1,0:T(8,128)(2,1)} %bitcast.11), calls=%async_computation.2 | async-start | bytes 1048576 | tf_op jit(solution)/shard_map/all_to_all | solution.py:64
  128.7 0.1 sqrt.8
  128.7 11.5 %all-to-all-done.2 = bf16[32,64,128]{2,1,0:T(8,128)(2,1)S(1)} async-done(((bf16[32,64,128]{2,1,0:T(8,128)(2,1)}), bf16[32,64,128]{2,1,0:T(8,128)(2,1)S(1)}, u32[]{:S(2)}, u32[]{:S(2)}) %all-to-all-start.2) | async-done | bytes 524320 | tf_op jit(solution)/shard_map/all_to_all | solution.py:64
  140.2 0.1 convert_reduce_fusion.1
  140.3 0.0 copy-done.1
  140.3 0.1 fusion.4
  140.4 12.6 %all_to_all.27 = bf16[16,64,128]{2,1,0:T(8,128)(2,1)S(1)} all-to-all(bf16[16,64,128]{2,1,0:T(8,128)(2,1)S(1)} %broadcast_in_dim.61), channel_id=1, replica_groups=mesh['xh'=2,'y'=4,'core'=2,'z'=16,'xl'=2] {'xh','y','xl'}, dimensions={0} | all-to-all | bytes 524288 | tf_op jit(solution)/shard_map/all_to_all | solution.py:20
  153.0 2.2 %all-gather.2 = bf16[32,64,128]{2,1,0:T(8,128)(2,1)S(1)} all-gather(bf16[16,64,128]{2,1,0:T(8,128)(2,1)S(1)} %all_to_all.27), channel_id=4, replica_groups=mesh['xh'=2,'y'=4,'core'=2,'z'=16,'xl'=2] {'core'}, dimensions={0}, use_global_device_ids=true | all-gather | bytes 786432 | tf_op jit(solution)/shard_map/all_gather | solution.py:69
  155.2 3.5 %convolution_convert_fusion.1 = bf16[1024,128]{1,0:T(8,128)(2,1)S(1)} fusion(bf16[2048,1024]{1,0:T(8,128)(2,1)} %get-tuple-element.17, bf16[2048,128]{1,0:T(8,128)(2,1)S(1)} %bitcast.44), kind=kOutput, calls=%fused_computation.4 | convolution fusion | flops 537001984 | bytes 4980736 | tf_op jit(solution)/shard_map/dot_general | solution.py:71
  158.7 22.3 %all_to_all.28 = bf16[16,64,128]{2,1,0:T(8,128)(2,1)S(1)} all-to-all(bf16[16,64,128]{2,1,0:T(8,128)(2,1)S(1)} %bitcast.46), channel_id=1, replica_groups=mesh['xh'=2,'y'=4,'core'=2,'z'=16,'xl'=2] {'z'}, dimensions={0} | all-to-all | bytes 524288 | tf_op jit(solution)/shard_map/all_to_all | solution.py:72
  181.0 0.7 select_add_fusion
  (11 shorter events, 0.2 us)
Async XLA Ops:
  6.5 43.5 %copy-start = (bf16[64,128]{1,0:T(8,128)(2,1)S(1)}, bf16[64,128]{1,0:T(8,128)(2,1)}, u32[]{:S(2)}) copy-start(bf16[64,128]{1,0:T(8,128)(2,1)} %param.5) | copy-start | bytes 49156
  6.5 40.7 %all-gather.5.cloned.1.call-start = ((), (), s32[]{:S(2)}) async-start(), calls=%async_computation.5 | async-start | bytes 1671168 | tf_op jit(solution)/shard_map/all_gather | solution.py:33
  95.2 45.0 %copy-start.1 = (s32[64]{0:T(128)S(1)}, s32[64]{0:T(128)}, u32[]{:S(2)}) copy-start(s32[64]{0:T(128)} %param.6) | copy-start | bytes 772
  121.6 18.6 %all-to-all-start.2 = ((bf16[32,64,128]{2,1,0:T(8,128)(2,1)}), bf16[32,64,128]{2,1,0:T(8,128)(2,1)S(1)}, u32[]{:S(2)}, u32[]{:S(2)}) async-start(bf16[32,64,128]{2,1,0:T(8,128)(2,1)} %bitcast.11), calls=%async_computation.2 | async-start | bytes 1048576 | tf_op jit(solution)/shard_map/all_to_all | solution.py:64
Sparse Core Ops, SparseCore 0:
  27.3 19.9 all-gather.4

commit v2 on v1

v2 whole, which is shorter than its diff:
```python
import functools

import jax
import jax.numpy as jnp
from jax import lax
from jax.experimental import pallas as pl
from jax.experimental.pallas import tpu as pltpu
from jax.sharding import Mesh, PartitionSpec as P

KERNEL_SPREAD = 0.05
PROPAGATE_WEIGHT = 0.9
SEED_WEIGHT = 0.1
RATE = 1.4426950408889634 / KERNEL_SPREAD
DROPPED = -1.0e30

AXES = ("xh", "y", "core", "z", "xl")
SIZES = (2, 4, 2, 16, 2)
ROW = ("xh", "y", "core")
COL = ("z", "xl")
PLANE = ("xh", "y", "xl")
LANES = 128
N = 64
A = 16 * N
H = 16 * N
BF = jnp.bfloat16
F32 = jnp.float32
PARAMS = pltpu.CompilerParams(vmem_limit_bytes=40 * 1024 * 1024)


def spread_gather(x, axes, count):
    copies = jnp.broadcast_to(x[None], (count,) + x.shape)
    return lax.all_to_all(copies, axes, 0, 0, tiled=True)


def similarity_kernel(column_ref, panel_ref, offset_ref, kernel_ref, sums_ref):
    for j in range(4):
        lo = panel_ref[4 * j : 4 * j + 4, :N, :].reshape(4 * N, LANES)
        hi = panel_ref[4 * j : 4 * j + 4, N : 2 * N, :].reshape(4 * N, LANES)
        right = jnp.concatenate([lo, hi], 1)
        sums = jnp.zeros((1, 4 * N), F32)
        for a in range(2):
            offset = jnp.concatenate(
                [offset_ref[a, 2 * j : 2 * j + 1, :], offset_ref[a, 2 * j + 1 : 2 * j + 2, :]], 1
            )
            for q in range(2):
                rows = 4 * (2 * a + q)
                lo = column_ref[rows : rows + 4, :N, :].reshape(4 * N, LANES)
                hi = column_ref[rows : rows + 4, N : 2 * N, :].reshape(4 * N, LANES)
                left = jnp.concatenate([lo, hi], 1)
                weights = lax.dot_general(
                    left, right, (((1,), (1,)), ((), ())), preferred_element_type=F32
                )
                tile = jnp.exp2(weights * RATE + offset).astype(BF)
                kernel_ref[rows * N : (rows + 4) * N, 4 * j * N : 4 * (j + 1) * N] = tile
                sums = sums + jnp.sum(tile.astype(F32), axis=0, keepdims=True)
        sums_ref[2 * j : 2 * j + 1, :] = sums[:, :LANES]
        sums_ref[2 * j + 1 : 2 * j + 2, :] = sums[:, LANES:]


def similarity(column, panel, offset):
    return pl.pallas_call(
        similarity_kernel,
        out_shape=(jax.ShapeDtypeStruct((A, H), BF), jax.ShapeDtypeStruct((8, LANES), F32)),
        compiler_params=PARAMS,
        cost_estimate=pl.CostEstimate(
            flops=2 * A * H * 256, bytes_accessed=4 << 20, transcendentals=A * H
        ),
        name="similarity",
    )(column, panel, offset)


def first_kernel(core_ref, parts_ref, prior0_ref, prior1_ref, k0_ref, k1_ref, out_ref, inv_ref):
    core = core_ref[0]
    total = None
    for side, (prior_ref, k_ref) in enumerate(((prior0_ref, k0_ref), (prior1_ref, k1_ref))):
        at = core if side == 0 else 1 - core
        inv = 1.0 / jnp.sqrt(jnp.sum(parts_ref[:, at], axis=0))
        inv_ref[at] = inv
        turned = inv.T
        scaled = []
        for k in range(8):
            prior = prior_ref[2 * k : 2 * k + 2].reshape(2 * N, LANES).astype(F32)
            scaled.append((turned[:, k : k + 1] * prior).astype(BF))
        scaled = jnp.concatenate(scaled, 0)
        part = jnp.dot(k_ref[...], scaled, preferred_element_type=F32)
        total = part if total is None else total + part
    out_ref[...] = total.astype(BF)


def first_product(core, parts, panel0, panel1, k0, k1):
    whole = lambda *shape: pl.BlockSpec(shape, lambda i: (0,) * len(shape))
    prior = pl.BlockSpec((16, N, LANES), lambda i: (0, 2, 0))
    return pl.pallas_call(
        first_kernel,
        grid=(1,),
        in_specs=[
            pl.BlockSpec(memory_space=pltpu.SMEM),
            whole(32, 2, 8, LANES),
            prior,
            prior,
            whole(A, H),
            whole(A, H),
        ],
        out_specs=(whole(A, LANES), whole(2, 8, LANES)),
        out_shape=(
            jax.ShapeDtypeStruct((A, LANES), BF),
            jax.ShapeDtypeStruct((2, 8, LANES), F32),
        ),
        compiler_params=PARAMS,
        cost_estimate=pl.CostEstimate(
            flops=4 * A * H * LANES, bytes_accessed=5 << 20, transcendentals=0
        ),
        name="first_product",
    )(core, parts, panel0, panel1, k0, k1)


def second_kernel(core_ref, scaled_ref, k0_ref, k1_ref, out_ref):
    core = core_ref[0]
    total = jnp.dot(k0_ref[...], scaled_ref[core].reshape(H, LANES), preferred_element_type=F32)
    total += jnp.dot(k1_ref[...], scaled_ref[1 - core].reshape(H, LANES), preferred_element_type=F32)
    out_ref[...] = total.astype(BF)


def second_product(core, scaled, k0, k1):
    vmem = pl.BlockSpec(memory_space=pltpu.VMEM)
    return pl.pallas_call(
        second_kernel,
        in_specs=[pl.BlockSpec(memory_space=pltpu.SMEM), vmem, vmem, vmem],
        out_shape=jax.ShapeDtypeStruct((A, LANES), BF),
        compiler_params=PARAMS,
        cost_estimate=pl.CostEstimate(
            flops=4 * A * H * LANES, bytes_accessed=5 << 20, transcendentals=0
        ),
        name="second_product",
    )(core, scaled, k0, k1)


def per_device(embeddings, prior_scores, seed_labels, tile_pattern):
    z, core = lax.axis_index("z"), lax.axis_index("core")
    halves = [embeddings[:, :LANES], embeddings[:, LANES:]]

    panel0 = spread_gather(jnp.concatenate(halves + [prior_scores], 0), PLANE, 16)

    flags = jnp.repeat(tile_pattern[:, 0].astype(BF), LANES // 2)
    flags = lax.all_gather(jnp.broadcast_to(flags[None, :], (8, LANES)), "xl", axis=0, tiled=True)
    column = lax.all_gather(jnp.concatenate(halves + [flags], 0), "z", axis=0)
    kept = column[:, 2 * N :: 8, :: LANES // 2]
    kept = lax.dynamic_index_in_dim(kept, z // 8, 1, False)
    offset = jnp.where(kept > 0, -RATE, DROPPED).astype(F32).reshape(8, 2, 2)
    offset = jnp.broadcast_to(offset.transpose(1, 2, 0)[..., None], (2, 2, 8, LANES))

    panel1 = lax.ppermute(panel0, "core", [(0, 1), (1, 0)])
    take = functools.partial(lax.dynamic_index_in_dim, axis=0, keepdims=False)
    kernel0, sums0 = similarity(column, panel0, take(offset, core))
    kernel1, sums1 = similarity(column, panel1, take(offset, 1 - core))

    sums = jnp.where(core == 0, jnp.stack([sums0, sums1]), jnp.stack([sums1, sums0]))
    parts = spread_gather(sums, ("core",) + PLANE, 32)
    core_word = core.astype(jnp.int32).reshape(1)
    part, inv = first_product(core_word, parts.reshape(32, 2, 8, LANES), panel0, panel1, kernel0, kernel1)
    inv_own = take(inv.reshape(32, N), lax.axis_index(("core",) + PLANE))[:, None]
    classes_iota = jnp.arange(LANES, dtype=jnp.int32)
    seeds = SEED_WEIGHT * (seed_labels[:, None] == classes_iota[None, :]).astype(F32)

    part = lax.all_to_all(part.reshape(16, N, LANES), "z", 0, 0, tiled=True)
    product = jnp.sum(part.astype(F32), axis=0)
    scores = PROPAGATE_WEIGHT * inv_own * product + seeds

    scaled = spread_gather((inv_own * scores).astype(BF), PLANE, 16)
    scaled = lax.all_gather(scaled, "core", axis=0)
    part = second_product(core_word, scaled, kernel0, kernel1)
    part = lax.all_to_all(part.reshape(16, N, LANES), "z", 0, 0, tiled=True)
    product = jnp.sum(part.astype(F32), axis=0)
    return PROPAGATE_WEIGHT * inv_own * product + seeds


def solution(mesh):
    return jax.shard_map(
        per_device,
        mesh=Mesh(mesh.devices.reshape(SIZES), AXES),
        in_specs=(P(AXES, None), P(AXES, None), P(AXES), P(ROW, COL)),
        out_specs=P(AXES, None),
        check_vma=False,
    )
```

time: 189 us -> 153 us (0.81)
  between operations: 13.5 us -> 0.17 us
  blocking collectives: 111 us -> 98.9 us
  matrix products: 12 us -> 0 us
  starting transfers between devices: 7.09 us -> 17.8 us
  waiting for transfers between devices: 31.5 us -> 21.8 us
  Pallas kernels: 0 us -> 7.78 us
  local copies, waits for them, and re-layouts: 11.1 us -> 4.41 us
    all_to_all x3 -> x2, blocking collectives: 53.5 us -> 25.1 us  [spread_gather(): return lax.all_to_all(copies, axes, 0, 0, tiled=True)]
    all_gather x1 -> x0, waiting for transfers between devices: 20.1 us -> none  [per_device(): panel = lax.all_gather(panel, 'core', axis=0)]
    all_gather x2 -> x3, blocking collectives: 35.7 us -> 49.4 us  [the longest x1 36.6 us: per_device(): column = lax.all_gather(jnp.concatenate(halves + [flags], 0), 'z', axis=0)]
    dot_general x3 -> x0, matrix products: 12 us -> none  [the longest x1 4.35 us: per_device(): part = jnp.dot(kernel, scaled_a, preferred_element_type=f32).astype(bf)]
    all_to_all x1 -> x2, waiting for transfers between devices: 11.5 us -> 21.8 us  [the longest x1 18.3 us: per_device(): part = lax.all_to_all(part.reshape(16, N, LANES), 'z', 0, 0, tiled=True)]
    all_to_all x1 -> x2, starting transfers between devices: 7.09 us -> 15.9 us  [the longest x1 8.85 us: per_device(): part = lax.all_to_all(part.reshape(16, N, LANES), 'z', 0, 0, tiled=True)]
    pallas_call x0 -> x4, Pallas kernels: none -> 7.78 us  [the longest x1 3.28 us: first_product(): pl.pallas_call(first_kernel, grid=(1,), in_specs=[pl.BlockSpec(memory_spa...]
    gt x4 -> x0, local copies, waits for them, and re-layouts: 5.09 us -> none  [per_device(): kernel = jnp.where(keep.reshape(kernel.shape) > 0, kernel, 0.0).astype(bf)]
  transfers between devices with their start and end apart: 2 -> 3, of which waited for: 2 -> 2; matrix products, arithmetic and copies ran while one was open for 0% -> 1% of each run, Pallas kernels for 0% -> 1%
where the time goes in v2:
time: 153 us; the launch traced here: 152 us
  blocking collectives  98.9 us (65%)
  waiting for transfers between devices  21.8 us (14%)
  starting transfers between devices  17.8 us (12%)
  Pallas kernels  7.78 us (5%)
  local copies, waits for them, and re-layouts  4.41 us (3%)
  other arithmetic  1.64 us (1%)
    all_gather x1, blocking collectives, per_device(): column = lax.all_gather(jnp.concatenate(halves + [flags], 0), 'z', axis=0)  36.6 us
    all_to_all x2, blocking collectives, spread_gather(): return lax.all_to_all(copies, axes, 0, 0, tiled=True)  25.1 us
    all_to_all x1, blocking collectives, per_device(): part = lax.all_to_all(part.reshape(16, N, LANES), 'z', 0, 0, tiled=True)  24.4 us
    all_to_all x1, waiting for transfers between devices, per_device(): part = lax.all_to_all(part.reshape(16, N, LANES), 'z', 0, 0, tiled=True)  18.3 us
    all_gather x1, blocking collectives, per_device(): lax.all_gather(jnp.broadcast_to(flags[None, :], (8, LANES)), 'xl', axis=0...  10.7 us
    all_to_all x1, starting transfers between devices, per_device(): part = lax.all_to_all(part.reshape(16, N, LANES), 'z', 0, 0, tiled=True)  8.85 us
    all_to_all x1, starting transfers between devices, spread_gather(): return lax.all_to_all(copies, axes, 0, 0, tiled=True)  7.03 us
    all_to_all x1, waiting for transfers between devices, spread_gather(): return lax.all_to_all(copies, axes, 0, 0, tiled=True)  3.52 us
  transfers between devices with their start and end apart: 3, of which 2 were waited for; matrix products, arithmetic and copies ran while one was open for 1% of the time, Pallas kernels for 1%

profile of v2, /device:TPU:32, one launch (start us, length us, event | category | flops | bytes accessed | tf_op | source)
XLA Modules:
  0.0 152.4 jit_solution(2692646990242027257)
XLA Ops:
  0.0 0.0 copy-start.3
  0.0 0.7 fusion.4
  0.8 0.7 pad_maximum_fusion
  1.5 1.0 broadcast_in_dim.56
  2.5 7.0 %all-to-all-start = ((bf16[16,192,128]{2,1,0:T(8,128)(2,1)}), bf16[16,192,128]{2,1,0:T(8,128)(2,1)S(1)}, u32[]{:S(2)}, u32[]{:S(2)}) async-start(bf16[16,192,128]{2,1,0:T(8,128)(2,1)} %broadcast_in_dim.56), calls=%async_computation | async-start | bytes 1572864 | tf_op jit(solution)/shard_map/all_to_all | solution.py:32
  9.6 0.0 copy-done.3
  9.6 0.1 broadcast_in_dim.53
  9.7 0.1 broadcast_in_dim.54
  9.7 10.7 %all_gather.15 = bf16[16,128]{1,0:T(8,128)(2,1)S(1)} all-gather(bf16[8,128]{1,0:T(8,128)(2,1)S(1)} %broadcast_in_dim.55), channel_id=1, replica_groups=mesh['xh'=2,'y'=4,'core'=2,'z'=16,'xl'=2] {'xl'}, dimensions={0}, use_global_device_ids=true | all-gather | bytes 6144 | tf_op jit(solution)/shard_map/all_gather | solution.py:145
  20.4 3.5 %all-to-all-done.panel_ref.prior0_ref = bf16[16,192,128]{2,1,0:T(8,128)(2,1)S(1)} async-done(((bf16[16,192,128]{2,1,0:T(8,128)(2,1)}), bf16[16,192,128]{2,1,0:T(8,128)(2,1)S(1)}, u32[]{:S(2)}, u32[]{:S(2)}) %all-to-all-start) | async-done | bytes 786464 | tf_op jit(solution)/shard_map/all_to_all | solution.py:32
  23.9 1.9 %collective-permute-start = (bf16[16,192,128]{2,1,0:T(8,128)(2,1)S(1)}, bf16[16,192,128]{2,1,0:T(8,128)(2,1)}, u32[]{:S(2)}, u32[]{:S(2)}) collective-permute-start(bf16[16,192,128]{2,1,0:T(8,128)(2,1)S(1)} %all-to-all-done.panel_ref.prior0_ref), channel_id=1, source_target_pairs={{0,32},{32,0},{1,33},{33,1},{2,34},{34,2},{3,35},{35,3},{4,36},{36... | collective-permute-start | bytes 2359304 | tf_op jit(solution)/shard_map/ppermute | solution.py:152
  25.9 36.6 %all-gather = bf16[2304,128]{1,0:T(8,128)(2,1)S(1)} all-gather(bf16[144,128]{1,0:T(8,128)(2,1)S(1)} %pad_maximum_fusion.1), channel_id=2, replica_groups=mesh['xh'=2,'y'=4,'core'=2,'z'=16,'xl'=2] {'z'}, dimensions={0}, use_global_device_ids=true | all-gather | bytes 626688 | tf_op jit(solution)/shard_map/all_gather | solution.py:146
  62.5 0.1 slice.11
  62.7 0.1 copy.9
  62.8 0.1 copy.10
  62.9 0.1 bitcast_reduce_fusion.1
  63.0 0.1 bitcast_reduce_fusion
  63.1 0.1 broadcast_in_dim.60.offset_ref
  63.2 1.1 similarity.2
  64.2 0.0 collective-permute-done.panel_ref.prior1_ref
  64.3 0.1 broadcast_in_dim.62.offset_ref
  64.3 2.2 %similarity.3 = (bf16[1024,1024]{1,0:T(8,128)(2,1)S(1)}, f32[8,128]{1,0:T(8,128)S(1)}) custom-call(bf16[16,144,128]{2,1,0:T(8,128)(2,1)S(1)} %bitcast.21, bf16[16,192,128]{2,1,0:T(8,128)(2,1)} %collective-permute-done.panel_ref.prior1_ref, f32[2,8,128]{2,1,0:T(8,128)S(1)} %broadcast_in_dim.62.offset_ref), custom_call_target="tpu_custom_call" | custom-call | flops 536870912 | bytes 4194304 | tf_op jit(solution)/shard_map/similarity/pallas_call | solution.py:61
  66.5 0.0 copy-start
  66.6 13.3 %all_to_all.25.parts_ref = f32[32,2,8,128]{3,2,1,0:T(8,128)S(1)} all-to-all(f32[32,2,8,128]{3,2,1,0:T(8,128)S(1)} %broadcast_in_dim.63), channel_id=1, replica_groups=mesh['xh'=2,'y'=4,'core'=2,'z'=16,'xl'=2] {'core','xh','y','xl'}, dimensions={0} | all-to-all | bytes 524288 | tf_op jit(solution)/shard_map/all_to_all | solution.py:32
  79.9 0.0 copy-start.2
  79.9 3.3 %first_product.1 = (bf16[1024,128]{1,0:T(8,128)(2,1)}, f32[2,8,128]{2,1,0:T(8,128)S(1)}) custom-call(s32[1]{0:T(128)} %bitcast.core_ref, f32[32,2,8,128]{3,2,1,0:T(8,128)S(1)} %all_to_all.25.parts_ref, bf16[16,192,128]{2,1,0:T(8,128)(2,1)S(1)} %all-to-all-done.panel_ref.prior0_ref, bf16[16,192,128]{2,1,0:T(8,128)(2,1)} %collective-permute-done.panel_ref.prior1_ref, ...), custom_call_target="tpu_custom_call" | custom-call | flops 536870912 | bytes 5242880 | tf_op jit(solution)/shard_map/first_product/pallas_call | solution.py:93
  83.2 0.0 copy-done
  83.2 8.9 %all-to-all-start.2 = ((bf16[16,64,128]{2,1,0:T(8,128)(2,1)}), bf16[16,64,128]{2,1,0:T(8,128)(2,1)S(1)}, u32[]{:S(2)}, u32[]{:S(2)}) async-start(bf16[16,64,128]{2,1,0:T(8,128)(2,1)} %bitcast.9), calls=%async_computation.2 | async-start | bytes 524288 | tf_op jit(solution)/shard_map/all_to_all | solution.py:165
  92.0 0.1 reshape.119
  92.1 18.3 %all-to-all-done.2 = bf16[16,64,128]{2,1,0:T(8,128)(2,1)S(1)} async-done(((bf16[16,64,128]{2,1,0:T(8,128)(2,1)}), bf16[16,64,128]{2,1,0:T(8,128)(2,1)S(1)}, u32[]{:S(2)}, u32[]{:S(2)}) %all-to-all-start.2) | async-done | bytes 262176 | tf_op jit(solution)/shard_map/all_to_all | solution.py:165
  110.4 0.0 copy-done.2
  110.4 0.1 fusion.1
  110.5 11.8 %all_to_all.26 = bf16[16,64,128]{2,1,0:T(8,128)(2,1)S(1)} all-to-all(bf16[16,64,128]{2,1,0:T(8,128)(2,1)S(1)} %broadcast_in_dim.65), channel_id=1, replica_groups=mesh['xh'=2,'y'=4,'core'=2,'z'=16,'xl'=2] {'xh','y','xl'}, dimensions={0} | all-to-all | bytes 524288 | tf_op jit(solution)/shard_map/all_to_all | solution.py:32
  122.3 2.2 %all-gather.1 = bf16[32,64,128]{2,1,0:T(8,128)(2,1)S(1)} all-gather(bf16[16,64,128]{2,1,0:T(8,128)(2,1)S(1)} %all_to_all.26), channel_id=3, replica_groups=mesh['xh'=2,'y'=4,'core'=2,'z'=16,'xl'=2] {'core'}, dimensions={0}, use_global_device_ids=true | all-gather | bytes 786432 | tf_op jit(solution)/shard_map/all_gather | solution.py:170
  124.5 0.0 copy-start.1
  124.5 1.6 %copy-done.1 = bf16[1024,1024]{1,0:T(8,128)(2,1)S(1)} copy-done((bf16[1024,1024]{1,0:T(8,128)(2,1)S(1)}, bf16[1024,1024]{1,0:T(8,128)(2,1)}, u32[]{:S(2)}) %copy-start.1) | copy-done | bytes 2097176
  126.1 1.2 second_product.1
  127.3 24.4 %all_to_all.27 = bf16[16,64,128]{2,1,0:T(8,128)(2,1)S(1)} all-to-all(bf16[16,64,128]{2,1,0:T(8,128)(2,1)S(1)} %bitcast.18), channel_id=1, replica_groups=mesh['xh'=2,'y'=4,'core'=2,'z'=16,'xl'=2] {'z'}, dimensions={0} | all-to-all | bytes 524288 | tf_op jit(solution)/shard_map/all_to_all | solution.py:172
  151.7 0.7 select_add_fusion
  (11 shorter events, 0.2 us)
Async XLA Ops:
  0.0 9.6 %copy-start.3 = (s32[2,1]{0,1:T(1,128)S(1)}, s32[2,1]{0,1:T(1,128)}, u32[]{:S(2)}) copy-start(s32[2,1]{0,1:T(1,128)} %param.7) | copy-start | bytes 28
  2.5 21.4 %all-to-all-start = ((bf16[16,192,128]{2,1,0:T(8,128)(2,1)}), bf16[16,192,128]{2,1,0:T(8,128)(2,1)S(1)}, u32[]{:S(2)}, u32[]{:S(2)}) async-start(bf16[16,192,128]{2,1,0:T(8,128)(2,1)} %broadcast_in_dim.56), calls=%async_computation | async-start | bytes 1572864 | tf_op jit(solution)/shard_map/all_to_all | solution.py:32
  23.9 40.3 %collective-permute-start = (bf16[16,192,128]{2,1,0:T(8,128)(2,1)S(1)}, bf16[16,192,128]{2,1,0:T(8,128)(2,1)}, u32[]{:S(2)}, u32[]{:S(2)}) collective-permute-start(bf16[16,192,128]{2,1,0:T(8,128)(2,1)S(1)} %all-to-all-done.panel_ref.prior0_ref), channel_id=1, source_target_pairs={{0,32},{32,0},{1,33},{33,1},{2,34},{34,2},{3,35},{35,3},{4,36},{36... | collective-permute-start | bytes 2359304 | tf_op jit(solution)/shard_map/ppermute | solution.py:152
  66.5 16.6 %copy-start = (bf16[1024,1024]{1,0:T(8,128)(2,1)}, bf16[1024,1024]{1,0:T(8,128)(2,1)S(1)}, u32[]{:S(2)}) copy-start(bf16[1024,1024]{1,0:T(8,128)(2,1)S(1)} %get-tuple-element.14.k1_ref) | copy-start | bytes 6291460
  79.9 30.5 %copy-start.2 = (s32[64]{0:T(128)S(1)}, s32[64]{0:T(128)}, u32[]{:S(2)}) copy-start(s32[64]{0:T(128)} %param.6) | copy-start | bytes 772
  83.2 27.2 %all-to-all-start.2 = ((bf16[16,64,128]{2,1,0:T(8,128)(2,1)}), bf16[16,64,128]{2,1,0:T(8,128)(2,1)S(1)}, u32[]{:S(2)}, u32[]{:S(2)}) async-start(bf16[16,64,128]{2,1,0:T(8,128)(2,1)} %bitcast.9), calls=%async_computation.2 | async-start | bytes 524288 | tf_op jit(solution)/shard_map/all_to_all | solution.py:165
  124.5 1.6 %copy-start.1 = (bf16[1024,1024]{1,0:T(8,128)(2,1)S(1)}, bf16[1024,1024]{1,0:T(8,128)(2,1)}, u32[]{:S(2)}) copy-start(bf16[1024,1024]{1,0:T(8,128)(2,1)} %copy-done) | copy-start | bytes 6291460

commit v3 on v2

v3 whole, which is shorter than its diff:
```python
import jax
import jax.numpy as jnp
from jax import lax
from jax.experimental import pallas as pl
from jax.experimental.pallas import tpu as pltpu
from jax.sharding import Mesh, PartitionSpec as P

KERNEL_SPREAD = 0.05
PROPAGATE_WEIGHT = 0.9
SEED_WEIGHT = 0.1
RATE = 1.4426950408889634 / KERNEL_SPREAD
DROPPED = -1.0e30

AXES = ("xh", "y", "core", "z", "xl")
SIZES = (2, 4, 2, 16, 2)
ROW = ("xh", "y", "core")
COL = ("z", "xl")
LANES = 128
N = 64
A = 16 * N
B = 32 * N
PLANE = ("core", "xh", "y", "xl")
BF = jnp.bfloat16
F32 = jnp.float32
PARAMS = pltpu.CompilerParams(vmem_limit_bytes=24 * 1024 * 1024)


def spread_gather(x, axes, count):
    copies = jnp.broadcast_to(x[None], (count,) + x.shape)
    return lax.all_to_all(copies, axes, 0, 0, tiled=True)


def similarity_kernel(column_ref, panel_ref, offset_ref, kernel_ref, sums_ref):
    for j in range(8):
        lo = panel_ref[4 * j : 4 * j + 4, :N, :].reshape(4 * N, LANES)
        hi = panel_ref[4 * j : 4 * j + 4, N : 2 * N, :].reshape(4 * N, LANES)
        right = jnp.concatenate([lo, hi], 1)
        sums = jnp.zeros((1, 4 * N), F32)
        for a in range(2):
            offset = jnp.concatenate(
                [offset_ref[a, 2 * j : 2 * j + 1, :], offset_ref[a, 2 * j + 1 : 2 * j + 2, :]], 1
            )
            for q in range(2):
                rows = 4 * (2 * a + q)
                lo = column_ref[rows : rows + 4, :N, :].reshape(4 * N, LANES)
                hi = column_ref[rows : rows + 4, N : 2 * N, :].reshape(4 * N, LANES)
                left = jnp.concatenate([lo, hi], 1)
                weights = lax.dot_general(
                    left, right, (((1,), (1,)), ((), ())), preferred_element_type=F32
                )
                tile = jnp.exp2(weights * RATE + offset).astype(BF)
                kernel_ref[rows * N : (rows + 4) * N, 4 * j * N : 4 * (j + 1) * N] = tile
                sums = sums + jnp.sum(tile.astype(F32), axis=0, keepdims=True)
        sums_ref[2 * j : 2 * j + 1, :] = sums[:, :LANES]
        sums_ref[2 * j + 1 : 2 * j + 2, :] = sums[:, LANES:]


def similarity(column, panel, offset):
    return pl.pallas_call(
        similarity_kernel,
        out_shape=(jax.ShapeDtypeStruct((A, B), BF), jax.ShapeDtypeStruct((16, LANES), F32)),
        compiler_params=PARAMS,
        cost_estimate=pl.CostEstimate(
            flops=2 * A * B * 256, bytes_accessed=4 << 20, transcendentals=A * B
        ),
        name="similarity",
    )(column, panel, offset)


def first_kernel(parts_ref, panel_ref, kernel_ref, out_ref, inv_ref):
    inv = 1.0 / jnp.sqrt(jnp.sum(parts_ref[...], axis=0))
    inv_ref[...] = inv
    turned = inv.T
    scaled = []
    for k in range(16):
        prior = panel_ref[2 * k : 2 * k + 2, 2 * N : 3 * N, :].reshape(2 * N, LANES).astype(F32)
        scaled.append((turned[:, k : k + 1] * prior).astype(BF))
    scaled = jnp.concatenate(scaled, 0)
    out_ref[...] = jnp.dot(kernel_ref[...], scaled, preferred_element_type=F32).astype(BF)


def first_product(parts, panel, kernel):
    return pl.pallas_call(
        first_kernel,
        out_shape=(
            jax.ShapeDtypeStruct((A, LANES), BF),
            jax.ShapeDtypeStruct((16, LANES), F32),
        ),
        compiler_params=PARAMS,
        cost_estimate=pl.CostEstimate(
            flops=2 * A * B * LANES, bytes_accessed=5 << 20, transcendentals=0
        ),
        name="first_product",
    )(parts, panel, kernel)


def second_kernel(scaled_ref, kernel_ref, out_ref):
    scaled = scaled_ref[...].reshape(B, LANES)
    out_ref[...] = jnp.dot(kernel_ref[...], scaled, preferred_element_type=F32).astype(BF)


def second_product(scaled, kernel):
    return pl.pallas_call(
        second_kernel,
        out_shape=jax.ShapeDtypeStruct((A, LANES), BF),
        compiler_params=PARAMS,
        cost_estimate=pl.CostEstimate(
            flops=2 * A * B * LANES, bytes_accessed=5 << 20, transcendentals=0
        ),
        name="second_product",
    )(scaled, kernel)


def per_device(embeddings, prior_scores, seed_labels, tile_pattern):
    z, xl = lax.axis_index("z"), lax.axis_index("xl")
    halves = [embeddings[:, :LANES], embeddings[:, LANES:]]

    flags = jnp.repeat(tile_pattern[:, 0].astype(BF), LANES // 2)
    flags = jnp.broadcast_to(flags[None, :], (8, LANES))
    other = lax.ppermute(flags, "xl", [(0, 1), (1, 0)])
    flags = [jnp.where(xl == 0, flags, other), jnp.where(xl == 0, other, flags)]

    panel = spread_gather(jnp.concatenate(halves + [prior_scores], 0), PLANE, 32)

    column = lax.all_gather(jnp.concatenate(halves + flags, 0), "z", axis=0)
    kept = column[:, 2 * N :: 8, :: LANES // 2]
    kept = lax.dynamic_index_in_dim(kept, z // 8, 1, False)
    offset = jnp.where(kept > 0, -RATE, DROPPED).astype(F32).reshape(8, 2, 2)
    offset = offset.transpose(2, 1, 0).reshape(2, 16)
    offset = jnp.broadcast_to(offset[..., None], (2, 16, LANES))

    kernel, sums = similarity(column, panel, offset)
    parts = spread_gather(sums, PLANE, 32)
    part, inv = first_product(parts, panel, kernel)
    inv_own = lax.dynamic_index_in_dim(inv.reshape(32, N), lax.axis_index(PLANE), 0, False)[:, None]
    classes_iota = jnp.arange(LANES, dtype=jnp.int32)
    seeds = SEED_WEIGHT * (seed_labels[:, None] == classes_iota[None, :]).astype(F32)

    part = lax.all_to_all(part.reshape(16, N, LANES), "z", 0, 0, tiled=True)
    product = jnp.sum(part.astype(F32), axis=0)
    scores = PROPAGATE_WEIGHT * inv_own * product + seeds

    scaled = spread_gather((inv_own * scores).astype(BF), PLANE[1:], 16)
    scaled = lax.all_gather(scaled, "core", axis=0)
    part = second_product(scaled, kernel)
    part = lax.all_to_all(part.reshape(16, N, LANES), "z", 0, 0, tiled=True)
    product = jnp.sum(part.astype(F32), axis=0)
    return PROPAGATE_WEIGHT * inv_own * product + seeds


def solution(mesh):
    return jax.shard_map(
        per_device,
        mesh=Mesh(mesh.devices.reshape(SIZES), AXES),
        in_specs=(P(AXES, None), P(AXES, None), P(AXES), P(ROW, COL)),
        out_specs=P(AXES, None),
        check_vma=False,
    )
```

time: 153 us -> 159 us (1.039)
  waiting for transfers between devices: 21.8 us -> 34.2 us
  blocking collectives: 98.9 us -> 91.4 us
  Pallas kernels: 7.78 us -> 5.41 us
  starting transfers between devices: 17.8 us -> 20 us
    ppermute x1, waiting for transfers between devices: 0.01 us -> 15.9 us  [per_device(): other = lax.ppermute(flags, 'xl', [(0, 1), (1, 0)])]
    all_gather x2 -> x1, blocking collectives: 47.3 us -> 36.6 us  [per_device(): column = lax.all_gather(jnp.concatenate(halves + flags, 0), 'z', axis=0)]
    all_to_all x1, waiting for transfers between devices: 3.52 us -> 0.01 us  [spread_gather(): return lax.all_to_all(copies, axes, 0, 0, tiled=True)]
    all_to_all x2, blocking collectives: 25.1 us -> 28.3 us  [spread_gather(): return lax.all_to_all(copies, axes, 0, 0, tiled=True)]
    pallas_call x4 -> x3, Pallas kernels: 7.78 us -> 5.41 us  [the longest x1 2.25 us: first_product(): pl.pallas_call(first_kernel, out_shape=(jax.ShapeDtypeStruct((A, LANES),...]
    ppermute x1, starting transfers between devices: 1.91 us -> 3.69 us  [per_device(): other = lax.ppermute(flags, 'xl', [(0, 1), (1, 0)])]
  transfers between devices with their start and end apart: 3 -> 3, of which waited for: 2 -> 2; matrix products, arithmetic and copies ran while one was open for 1% -> 0% of each run, Pallas kernels for 1% -> 0%
where the time goes in v3:
time: 159 us; the launch traced here: 158 us
  blocking collectives  91.4 us (57%)
  waiting for transfers between devices  34.2 us (22%)
  starting transfers between devices  20 us (13%)
  Pallas kernels  5.41 us (3%)
  local copies, waits for them, and re-layouts  5.24 us (3%)
  other arithmetic  1.64 us (1%)
    all_gather x1, blocking collectives, per_device(): column = lax.all_gather(jnp.concatenate(halves + flags, 0), 'z', axis=0)  36.6 us
    all_to_all x2, blocking collectives, spread_gather(): return lax.all_to_all(copies, axes, 0, 0, tiled=True)  28.3 us
    all_to_all x1, blocking collectives, per_device(): part = lax.all_to_all(part.reshape(16, N, LANES), 'z', 0, 0, tiled=True)  24.4 us
    all_to_all x1, waiting for transfers between devices, per_device(): part = lax.all_to_all(part.reshape(16, N, LANES), 'z', 0, 0, tiled=True)  18.2 us
    ppermute x1, waiting for transfers between devices, per_device(): other = lax.ppermute(flags, 'xl', [(0, 1), (1, 0)])  15.9 us
    all_to_all x1, starting transfers between devices, per_device(): part = lax.all_to_all(part.reshape(16, N, LANES), 'z', 0, 0, tiled=True)  8.84 us
    all_to_all x1, starting transfers between devices, spread_gather(): return lax.all_to_all(copies, axes, 0, 0, tiled=True)  7.45 us
    ppermute x1, starting transfers between devices, per_device(): other = lax.ppermute(flags, 'xl', [(0, 1), (1, 0)])  3.69 us
  transfers between devices with their start and end apart: 3, of which 2 were waited for; matrix products, arithmetic and copies ran while one was open for 0% of the time, Pallas kernels for 0%

profile of v3, /device:TPU:32, one launch (start us, length us, event | category | flops | bytes accessed | tf_op | source)
XLA Modules:
  0.0 158.0 jit_solution(1875203687213650084)
XLA Ops:
  0.0 0.7 fusion.2
  0.7 0.7 pad_maximum_fusion
  1.5 1.5 broadcast_in_dim.51
  3.0 0.0 copy-start.3
  3.0 7.5 %all-to-all-start = ((bf16[32,192,128]{2,1,0:T(8,128)(2,1)}), bf16[32,192,128]{2,1,0:T(8,128)(2,1)S(1)}, u32[]{:S(2)}, u32[]{:S(2)}) async-start(bf16[32,192,128]{2,1,0:T(8,128)(2,1)} %broadcast_in_dim.51), calls=%async_computation | async-start | bytes 3145728 | tf_op jit(solution)/shard_map/all_to_all | solution.py:30
  10.4 0.0 copy-done.3
  10.4 0.1 broadcast_in_dim.48
  10.5 0.1 broadcast_in_dim.49
  10.6 3.7 %collective-permute-start = (bf16[8,128]{1,0:T(8,128)(2,1)S(1)}, bf16[8,128]{1,0:T(8,128)(2,1)S(1)}, u32[]{:S(2)}, u32[]{:S(2)}) collective-permute-start(bf16[8,128]{1,0:T(8,128)(2,1)S(1)} %broadcast_in_dim.50), channel_id=1, source_target_pairs={{0,1},{1,0},{2,3},{3,2},{4,5},{5,4},{6,7},{7,6},{8,9},{9,8},{10,11... | collective-permute-start | bytes 6152 | tf_op jit(solution)/shard_map/ppermute | solution.py:120
  14.3 15.9 %collective-permute-done = bf16[8,128]{1,0:T(8,128)(2,1)S(1)} collective-permute-done((bf16[8,128]{1,0:T(8,128)(2,1)S(1)}, bf16[8,128]{1,0:T(8,128)(2,1)S(1)}, u32[]{:S(2)}, u32[]{:S(2)}) %collective-permute-start) | collective-permute-done | bytes 2080 | tf_op jit(solution)/shard_map/ppermute | solution.py:120
  30.3 36.6 %all-gather = bf16[2304,128]{1,0:T(8,128)(2,1)S(1)} all-gather(bf16[144,128]{1,0:T(8,128)(2,1)S(1)} %pad_maximum_fusion.1), channel_id=2, replica_groups=mesh['xh'=2,'y'=4,'core'=2,'z'=16,'xl'=2] {'z'}, dimensions={0}, use_global_device_ids=true | all-gather | bytes 626688 | tf_op jit(solution)/shard_map/all_gather | solution.py:125
  66.9 0.1 slice.11
  67.0 0.1 copy.11
  67.1 0.1 copy.10
  67.2 0.1 broadcast_in_dim.54
  67.3 0.0 all-to-all-done.panel_ref
  67.3 0.1 broadcast_in_dim.55.offset_ref
  67.4 1.9 %similarity.1 = (bf16[1024,2048]{1,0:T(8,128)(2,1)S(1)}, f32[16,128]{1,0:T(8,128)S(1)}) custom-call(bf16[16,144,128]{2,1,0:T(8,128)(2,1)S(1)} %bitcast.14, bf16[32,192,128]{2,1,0:T(8,128)(2,1)S(1)} %all-to-all-done.panel_ref, f32[2,16,128]{2,1,0:T(8,128)S(1)} %broadcast_in_dim.55.offset_ref), custom_call_target="tpu_custom_call" | custom-call | flops 1073741824 | bytes 4194304 | tf_op jit(solution)/shard_map/similarity/pallas_call | solution.py:59
  69.3 0.0 copy-start
  69.4 16.5 %all_to_all.25.parts_ref = f32[32,16,128]{2,1,0:T(8,128)S(1)} all-to-all(f32[32,16,128]{2,1,0:T(8,128)S(1)} %broadcast_in_dim.56), channel_id=1, replica_groups=mesh['xh'=2,'y'=4,'core'=2,'z'=16,'xl'=2] {'core','xh','y','xl'}, dimensions={0} | all-to-all | bytes 524288 | tf_op jit(solution)/shard_map/all_to_all | solution.py:30
  85.9 0.0 copy-start.2
  85.9 2.2 %first_product.1 = (bf16[1024,128]{1,0:T(8,128)(2,1)}, f32[16,128]{1,0:T(8,128)S(1)}) custom-call(f32[32,16,128]{2,1,0:T(8,128)S(1)} %all_to_all.25.parts_ref, bf16[32,192,128]{2,1,0:T(8,128)(2,1)S(1)} %all-to-all-done.panel_ref, bf16[1024,2048]{1,0:T(8,128)(2,1)S(1)} %get-tuple-element.10.kernel_ref), custom_call_target="tpu_custom_call" | custom-call | flops 536870912 | bytes 5242880 | tf_op jit(solution)/shard_map/first_product/pallas_call | solution.py:83
  88.1 0.0 copy-done
  88.1 8.8 %all-to-all-start.2 = ((bf16[16,64,128]{2,1,0:T(8,128)(2,1)}), bf16[16,64,128]{2,1,0:T(8,128)(2,1)S(1)}, u32[]{:S(2)}, u32[]{:S(2)}) async-start(bf16[16,64,128]{2,1,0:T(8,128)(2,1)} %bitcast.5), calls=%async_computation.2 | async-start | bytes 524288 | tf_op jit(solution)/shard_map/all_to_all | solution.py:139
  97.0 0.1 reshape.79
  97.1 18.2 %all-to-all-done.2 = bf16[16,64,128]{2,1,0:T(8,128)(2,1)S(1)} async-done(((bf16[16,64,128]{2,1,0:T(8,128)(2,1)}), bf16[16,64,128]{2,1,0:T(8,128)(2,1)S(1)}, u32[]{:S(2)}, u32[]{:S(2)}) %all-to-all-start.2) | async-done | bytes 262176 | tf_op jit(solution)/shard_map/all_to_all | solution.py:139
  115.3 0.0 copy-done.2
  115.3 0.1 fusion.1
  115.5 11.8 %all_to_all.26 = bf16[16,64,128]{2,1,0:T(8,128)(2,1)S(1)} all-to-all(bf16[16,64,128]{2,1,0:T(8,128)(2,1)S(1)} %broadcast_in_dim.58), channel_id=1, replica_groups=mesh['xh'=2,'y'=4,'core'=2,'z'=16,'xl'=2] {'xh','y','xl'}, dimensions={0} | all-to-all | bytes 524288 | tf_op jit(solution)/shard_map/all_to_all | solution.py:30
  127.3 2.2 %all-gather.1 = bf16[32,64,128]{2,1,0:T(8,128)(2,1)S(1)} all-gather(bf16[16,64,128]{2,1,0:T(8,128)(2,1)S(1)} %all_to_all.26), channel_id=3, replica_groups=mesh['xh'=2,'y'=4,'core'=2,'z'=16,'xl'=2] {'core'}, dimensions={0}, use_global_device_ids=true | all-gather | bytes 786432 | tf_op jit(solution)/shard_map/all_gather | solution.py:144
  129.4 0.0 copy-start.1
  129.4 2.2 %copy-done.1 = bf16[1024,2048]{1,0:T(8,128)(2,1)S(1)} copy-done((bf16[1024,2048]{1,0:T(8,128)(2,1)S(1)}, bf16[1024,2048]{1,0:T(8,128)(2,1)}, u32[]{:S(2)}) %copy-start.1) | copy-done | bytes 4194328
  131.6 1.2 second_product.1
  132.9 24.4 %all_to_all.27 = bf16[16,64,128]{2,1,0:T(8,128)(2,1)S(1)} all-to-all(bf16[16,64,128]{2,1,0:T(8,128)(2,1)S(1)} %bitcast.12), channel_id=1, replica_groups=mesh['xh'=2,'y'=4,'core'=2,'z'=16,'xl'=2] {'z'}, dimensions={0} | all-to-all | bytes 524288 | tf_op jit(solution)/shard_map/all_to_all | solution.py:146
  157.3 0.7 select_add_fusion
  (10 shorter events, 0.2 us)
Async XLA Ops:
  3.0 7.5 %copy-start.3 = (s32[2,1]{0,1:T(1,128)S(1)}, s32[2,1]{0,1:T(1,128)}, u32[]{:S(2)}) copy-start(s32[2,1]{0,1:T(1,128)} %param.7) | copy-start | bytes 28
  3.0 64.4 %all-to-all-start = ((bf16[32,192,128]{2,1,0:T(8,128)(2,1)}), bf16[32,192,128]{2,1,0:T(8,128)(2,1)S(1)}, u32[]{:S(2)}, u32[]{:S(2)}) async-start(bf16[32,192,128]{2,1,0:T(8,128)(2,1)} %broadcast_in_dim.51), calls=%async_computation | async-start | bytes 3145728 | tf_op jit(solution)/shard_map/all_to_all | solution.py:30
  10.6 19.6 %collective-permute-start = (bf16[8,128]{1,0:T(8,128)(2,1)S(1)}, bf16[8,128]{1,0:T(8,128)(2,1)S(1)}, u32[]{:S(2)}, u32[]{:S(2)}) collective-permute-start(bf16[8,128]{1,0:T(8,128)(2,1)S(1)} %broadcast_in_dim.50), channel_id=1, source_target_pairs={{0,1},{1,0},{2,3},{3,2},{4,5},{5,4},{6,7},{7,6},{8,9},{9,8},{10,11... | collective-permute-start | bytes 6152 | tf_op jit(solution)/shard_map/ppermute | solution.py:120
  69.3 18.8 %copy-start = (bf16[1024,2048]{1,0:T(8,128)(2,1)}, bf16[1024,2048]{1,0:T(8,128)(2,1)S(1)}, u32[]{:S(2)}) copy-start(bf16[1024,2048]{1,0:T(8,128)(2,1)S(1)} %get-tuple-element.10.kernel_ref) | copy-start | bytes 12582916
  85.9 29.5 %copy-start.2 = (s32[64]{0:T(128)S(1)}, s32[64]{0:T(128)}, u32[]{:S(2)}) copy-start(s32[64]{0:T(128)} %param.6) | copy-start | bytes 772
  88.1 27.2 %all-to-all-start.2 = ((bf16[16,64,128]{2,1,0:T(8,128)(2,1)}), bf16[16,64,128]{2,1,0:T(8,128)(2,1)S(1)}, u32[]{:S(2)}, u32[]{:S(2)}) async-start(bf16[16,64,128]{2,1,0:T(8,128)(2,1)} %bitcast.5), calls=%async_computation.2 | async-start | bytes 524288 | tf_op jit(solution)/shard_map/all_to_all | solution.py:139
  129.4 2.2 %copy-start.1 = (bf16[1024,2048]{1,0:T(8,128)(2,1)S(1)}, bf16[1024,2048]{1,0:T(8,128)(2,1)}, u32[]{:S(2)}) copy-start(bf16[1024,2048]{1,0:T(8,128)(2,1)} %copy-done) | copy-start | bytes 12582916

commit v4 on v3

--- a/solution.py
+++ b/solution.py
@@ -120,7 +120,9 @@
     other = lax.ppermute(flags, "xl", [(0, 1), (1, 0)])
     flags = [jnp.where(xl == 0, flags, other), jnp.where(xl == 0, other, flags)]
 
-    panel = spread_gather(jnp.concatenate(halves + [prior_scores], 0), PLANE, 32)
+    load = jnp.concatenate(halves + [prior_scores], 0)
+    flags, load = lax.optimization_barrier((flags, load))
+    panel = spread_gather(load, PLANE, 32)
 
     column = lax.all_gather(jnp.concatenate(halves + flags, 0), "z", axis=0)
     kept = column[:, 2 * N :: 8, :: LANES // 2]

time: 159 us -> 143 us (0.90)
  waiting for transfers between devices: 34.2 us -> 18.9 us
    ppermute x1, waiting for transfers between devices: 15.9 us -> 0.61 us  [per_device(): other = lax.ppermute(flags, 'xl', [(0, 1), (1, 0)])]
  transfers between devices with their start and end apart: 3 -> 3, of which waited for: 2 -> 2; matrix products, arithmetic and copies ran while one was open for 0% -> 1% of each run, Pallas kernels for 0% -> 0%
where the time goes in v4:
time: 143 us
  blocking collectives  91.4 us (64%)
  starting transfers between devices  19.6 us (14%)
  waiting for transfers between devices  18.9 us (13%)
  Pallas kernels  5.41 us (4%)
  local copies, waits for them, and re-layouts  5.24 us (4%)
  other arithmetic  2.29 us (2%)
    all_gather x1, blocking collectives, per_device(): column = lax.all_gather(jnp.concatenate(halves + flags, 0), 'z', axis=0)  36.5 us
    all_to_all x2, blocking collectives, spread_gather(): return lax.all_to_all(copies, axes, 0, 0, tiled=True)  28.3 us
    all_to_all x1, blocking collectives, per_device(): part = lax.all_to_all(part.reshape(16, N, LANES), 'z', 0, 0, tiled=True)  24.4 us
    all_to_all x1, waiting for transfers between devices, per_device(): part = lax.all_to_all(part.reshape(16, N, LANES), 'z', 0, 0, tiled=True)  18.2 us
    all_to_all x1, starting transfers between devices, per_device(): part = lax.all_to_all(part.reshape(16, N, LANES), 'z', 0, 0, tiled=True)  8.88 us
    all_to_all x1, starting transfers between devices, spread_gather(): return lax.all_to_all(copies, axes, 0, 0, tiled=True)  7.32 us
    ppermute x1, starting transfers between devices, per_device(): other = lax.ppermute(flags, 'xl', [(0, 1), (1, 0)])  3.39 us
  transfers between devices with their start and end apart: 3, of which 2 were waited for; matrix products, arithmetic and copies ran while one was open for 1% of the time, Pallas kernels for 0%

profile of v4, /device:TPU:32, one launch (start us, length us, event | category | flops | bytes accessed | tf_op | source)
XLA Modules:
  0.0 142.9 jit_solution(17239897134700220688)
XLA Ops:
  0.0 0.7 convert_bitcast_fusion
  0.7 0.1 broadcast_in_dim.48
  0.7 0.1 broadcast_in_dim.49
  0.8 3.4 %collective-permute-start = (bf16[8,128]{1,0:T(8,128)(2,1)S(1)}, bf16[8,128]{1,0:T(8,128)(2,1)S(1)}, u32[]{:S(2)}, u32[]{:S(2)}) collective-permute-start(bf16[8,128]{1,0:T(8,128)(2,1)S(1)} %broadcast_in_dim.50), channel_id=1, source_target_pairs={{0,1},{1,0},{2,3},{3,2},{4,5},{5,4},{6,7},{7,6},{8,9},{9,8},{10,11... | collective-permute-start | bytes 6152 | tf_op jit(solution)/shard_map/ppermute | solution.py:120
  4.2 0.7 fusion.2
  5.0 0.7 pad_maximum_fusion
  5.7 0.6 collective-permute-done
  6.3 1.5 %broadcast_in_dim.51 = bf16[32,192,128]{2,1,0:T(8,128)(2,1)} broadcast(bf16[192,128]{1,0:T(8,128)(2,1)S(1)} %pad_maximum_fusion), dimensions={1,2} | broadcast | bytes 1622016 | tf_op jit(solution)/shard_map/broadcast_in_dim | solution.py:29
  7.8 7.3 %all-to-all-start = ((bf16[32,192,128]{2,1,0:T(8,128)(2,1)}), bf16[32,192,128]{2,1,0:T(8,128)(2,1)S(1)}, u32[]{:S(2)}, u32[]{:S(2)}) async-start(bf16[32,192,128]{2,1,0:T(8,128)(2,1)} %broadcast_in_dim.51), calls=%async_computation | async-start | bytes 3145728 | tf_op jit(solution)/shard_map/all_to_all | solution.py:30
  15.2 36.5 %all-gather = bf16[2304,128]{1,0:T(8,128)(2,1)S(1)} all-gather(bf16[144,128]{1,0:T(8,128)(2,1)S(1)} %pad_maximum_fusion.1), channel_id=2, replica_groups=mesh['xh'=2,'y'=4,'core'=2,'z'=16,'xl'=2] {'z'}, dimensions={0}, use_global_device_ids=true | all-gather | bytes 626688 | tf_op jit(solution)/shard_map/all_gather | solution.py:127
  51.7 0.1 slice.11
  51.9 0.1 copy.11
  52.0 0.1 copy.10
  52.1 0.1 broadcast_in_dim.54
  52.2 0.0 all-to-all-done.panel_ref
  52.2 0.1 broadcast_in_dim.55.offset_ref
  52.2 1.9 %similarity.1 = (bf16[1024,2048]{1,0:T(8,128)(2,1)S(1)}, f32[16,128]{1,0:T(8,128)S(1)}) custom-call(bf16[16,144,128]{2,1,0:T(8,128)(2,1)S(1)} %bitcast.14, bf16[32,192,128]{2,1,0:T(8,128)(2,1)S(1)} %all-to-all-done.panel_ref, f32[2,16,128]{2,1,0:T(8,128)S(1)} %broadcast_in_dim.55.offset_ref), custom_call_target="tpu_custom_call" | custom-call | flops 1073741824 | bytes 4194304 | tf_op jit(solution)/shard_map/similarity/pallas_call | solution.py:59
  54.2 0.0 copy-start
  54.2 16.5 %all_to_all.25.parts_ref = f32[32,16,128]{2,1,0:T(8,128)S(1)} all-to-all(f32[32,16,128]{2,1,0:T(8,128)S(1)} %broadcast_in_dim.56), channel_id=1, replica_groups=mesh['xh'=2,'y'=4,'core'=2,'z'=16,'xl'=2] {'core','xh','y','xl'}, dimensions={0} | all-to-all | bytes 524288 | tf_op jit(solution)/shard_map/all_to_all | solution.py:30
  70.7 0.0 copy-start.2
  70.7 2.2 %first_product.1 = (bf16[1024,128]{1,0:T(8,128)(2,1)}, f32[16,128]{1,0:T(8,128)S(1)}) custom-call(f32[32,16,128]{2,1,0:T(8,128)S(1)} %all_to_all.25.parts_ref, bf16[32,192,128]{2,1,0:T(8,128)(2,1)S(1)} %all-to-all-done.panel_ref, bf16[1024,2048]{1,0:T(8,128)(2,1)S(1)} %get-tuple-element.16.kernel_ref), custom_call_target="tpu_custom_call" | custom-call | flops 536870912 | bytes 5242880 | tf_op jit(solution)/shard_map/first_product/pallas_call | solution.py:83
  73.0 0.0 copy-done
  73.0 8.9 %all-to-all-start.2 = ((bf16[16,64,128]{2,1,0:T(8,128)(2,1)}), bf16[16,64,128]{2,1,0:T(8,128)(2,1)S(1)}, u32[]{:S(2)}, u32[]{:S(2)}) async-start(bf16[16,64,128]{2,1,0:T(8,128)(2,1)} %bitcast.5), calls=%async_computation.2 | async-start | bytes 524288 | tf_op jit(solution)/shard_map/all_to_all | solution.py:141
  81.9 0.1 reshape.79
  81.9 18.2 %all-to-all-done.2 = bf16[16,64,128]{2,1,0:T(8,128)(2,1)S(1)} async-done(((bf16[16,64,128]{2,1,0:T(8,128)(2,1)}), bf16[16,64,128]{2,1,0:T(8,128)(2,1)S(1)}, u32[]{:S(2)}, u32[]{:S(2)}) %all-to-all-start.2) | async-done | bytes 262176 | tf_op jit(solution)/shard_map/all_to_all | solution.py:141
  100.2 0.0 copy-done.2
  100.2 0.1 fusion.1
  100.4 11.8 %all_to_all.26 = bf16[16,64,128]{2,1,0:T(8,128)(2,1)S(1)} all-to-all(bf16[16,64,128]{2,1,0:T(8,128)(2,1)S(1)} %broadcast_in_dim.58), channel_id=1, replica_groups=mesh['xh'=2,'y'=4,'core'=2,'z'=16,'xl'=2] {'xh','y','xl'}, dimensions={0} | all-to-all | bytes 524288 | tf_op jit(solution)/shard_map/all_to_all | solution.py:30
  112.2 2.2 %all-gather.1 = bf16[32,64,128]{2,1,0:T(8,128)(2,1)S(1)} all-gather(bf16[16,64,128]{2,1,0:T(8,128)(2,1)S(1)} %all_to_all.26), channel_id=3, replica_groups=mesh['xh'=2,'y'=4,'core'=2,'z'=16,'xl'=2] {'core'}, dimensions={0}, use_global_device_ids=true | all-gather | bytes 786432 | tf_op jit(solution)/shard_map/all_gather | solution.py:146
  114.3 0.0 copy-start.1
  114.3 2.2 %copy-done.1 = bf16[1024,2048]{1,0:T(8,128)(2,1)S(1)} copy-done((bf16[1024,2048]{1,0:T(8,128)(2,1)S(1)}, bf16[1024,2048]{1,0:T(8,128)(2,1)}, u32[]{:S(2)}) %copy-start.1) | copy-done | bytes 4194328
  116.5 1.2 second_product.1
  117.8 24.4 %all_to_all.27 = bf16[16,64,128]{2,1,0:T(8,128)(2,1)S(1)} all-to-all(bf16[16,64,128]{2,1,0:T(8,128)(2,1)S(1)} %bitcast.12), channel_id=1, replica_groups=mesh['xh'=2,'y'=4,'core'=2,'z'=16,'xl'=2] {'z'}, dimensions={0} | all-to-all | bytes 524288 | tf_op jit(solution)/shard_map/all_to_all | solution.py:148
  142.2 0.7 select_add_fusion
  (9 shorter events, 0.2 us)
Async XLA Ops:
  0.8 5.5 %collective-permute-start = (bf16[8,128]{1,0:T(8,128)(2,1)S(1)}, bf16[8,128]{1,0:T(8,128)(2,1)S(1)}, u32[]{:S(2)}, u32[]{:S(2)}) collective-permute-start(bf16[8,128]{1,0:T(8,128)(2,1)S(1)} %broadcast_in_dim.50), channel_id=1, source_target_pairs={{0,1},{1,0},{2,3},{3,2},{4,5},{5,4},{6,7},{7,6},{8,9},{9,8},{10,11... | collective-permute-start | bytes 6152 | tf_op jit(solution)/shard_map/ppermute | solution.py:120
  7.8 44.4 %all-to-all-start = ((bf16[32,192,128]{2,1,0:T(8,128)(2,1)}), bf16[32,192,128]{2,1,0:T(8,128)(2,1)S(1)}, u32[]{:S(2)}, u32[]{:S(2)}) async-start(bf16[32,192,128]{2,1,0:T(8,128)(2,1)} %broadcast_in_dim.51), calls=%async_computation | async-start | bytes 3145728 | tf_op jit(solution)/shard_map/all_to_all | solution.py:30
  54.2 18.8 %copy-start = (bf16[1024,2048]{1,0:T(8,128)(2,1)}, bf16[1024,2048]{1,0:T(8,128)(2,1)S(1)}, u32[]{:S(2)}) copy-start(bf16[1024,2048]{1,0:T(8,128)(2,1)S(1)} %get-tuple-element.16.kernel_ref) | copy-start | bytes 12582916
  70.7 29.5 %copy-start.2 = (s32[64]{0:T(128)S(1)}, s32[64]{0:T(128)}, u32[]{:S(2)}) copy-start(s32[64]{0:T(128)} %param.6) | copy-start | bytes 772
  73.0 27.2 %all-to-all-start.2 = ((bf16[16,64,128]{2,1,0:T(8,128)(2,1)}), bf16[16,64,128]{2,1,0:T(8,128)(2,1)S(1)}, u32[]{:S(2)}, u32[]{:S(2)}) async-start(bf16[16,64,128]{2,1,0:T(8,128)(2,1)} %bitcast.5), calls=%async_computation.2 | async-start | bytes 524288 | tf_op jit(solution)/shard_map/all_to_all | solution.py:141
  114.3 2.2 %copy-start.1 = (bf16[1024,2048]{1,0:T(8,128)(2,1)S(1)}, bf16[1024,2048]{1,0:T(8,128)(2,1)}, u32[]{:S(2)}) copy-start(bf16[1024,2048]{1,0:T(8,128)(2,1)} %copy-done) | copy-start | bytes 12582916

commit v5 on v3

--- a/solution.py
+++ b/solution.py
@@ -30,16 +30,41 @@
     return lax.all_to_all(copies, axes, 0, 0, tiled=True)
 
 
-def similarity_kernel(column_ref, panel_ref, offset_ref, kernel_ref, sums_ref):
+def load_kernel(emb_ref, prior_ref, copies_ref, stacked_ref):
+    emb = jnp.concatenate([emb_ref[:, :LANES], emb_ref[:, LANES:]], 0)
+    stacked_ref[...] = emb
+    rows = jnp.concatenate([emb, prior_ref[...]], 0)
+    for i in range(32):
+        copies_ref[i] = rows
+
+
+def make_loads(embeddings, prior_scores):
+    return pl.pallas_call(
+        load_kernel,
+        out_shape=(
+            jax.ShapeDtypeStruct((32, 3 * N, LANES), BF),
+            jax.ShapeDtypeStruct((2 * N, LANES), BF),
+        ),
+        compiler_params=PARAMS,
+        cost_estimate=pl.CostEstimate(flops=0, bytes_accessed=4 << 20, transcendentals=0),
+        name="make_loads",
+    )(embeddings, prior_scores)
+
+
+def similarity_kernel(half_ref, column_ref, panel_ref, kernel_ref, sums_ref):
+    offsets = []
+    for b in range(16):
+        flags = column_ref[(b % 8) * 2 + b // 8, 2 * N :, :].astype(F32)
+        flags = jnp.where(half_ref[0] == 0, flags[:8], flags[8:])
+        offsets.append(jnp.where(flags > 0.5, -RATE, DROPPED))
     for j in range(8):
         lo = panel_ref[4 * j : 4 * j + 4, :N, :].reshape(4 * N, LANES)
         hi = panel_ref[4 * j : 4 * j + 4, N : 2 * N, :].reshape(4 * N, LANES)
         right = jnp.concatenate([lo, hi], 1)
         sums = jnp.zeros((1, 4 * N), F32)
         for a in range(2):
-            offset = jnp.concatenate(
-                [offset_ref[a, 2 * j : 2 * j + 1, :], offset_ref[a, 2 * j + 1 : 2 * j + 2, :]], 1
-            )
+            row = slice(4 * a, 4 * a + 1)
+            offset = jnp.concatenate([offsets[2 * j][row], offsets[2 * j + 1][row]], 1)
             for q in range(2):
                 rows = 4 * (2 * a + q)
                 lo = column_ref[rows : rows + 4, :N, :].reshape(4 * N, LANES)
@@ -55,16 +80,18 @@
         sums_ref[2 * j + 1 : 2 * j + 2, :] = sums[:, LANES:]
 
 
-def similarity(column, panel, offset):
+def similarity(half, column, panel):
+    vmem = pl.BlockSpec(memory_space=pltpu.VMEM)
     return pl.pallas_call(
         similarity_kernel,
+        in_specs=[pl.BlockSpec(memory_space=pltpu.SMEM), vmem, vmem],
         out_shape=(jax.ShapeDtypeStruct((A, B), BF), jax.ShapeDtypeStruct((16, LANES), F32)),
         compiler_params=PARAMS,
         cost_estimate=pl.CostEstimate(
             flops=2 * A * B * 256, bytes_accessed=4 << 20, transcendentals=A * B
         ),
         name="similarity",
-    )(column, panel, offset)
+    )(half, column, panel)
 
 
 def first_kernel(parts_ref, panel_ref, kernel_ref, out_ref, inv_ref):
@@ -94,16 +121,36 @@
     )(parts, panel, kernel)
 
 
-def second_kernel(scaled_ref, kernel_ref, out_ref):
+PIECES = 8
+ROWS = A // PIECES
+
+
+def second_kernel(scaled_ref, kernel_ref, out_ref, held, sems):
+    copies = [
+        pltpu.make_async_copy(
+            kernel_ref.at[pl.ds(i * ROWS, ROWS)], held.at[pl.ds(i * ROWS, ROWS)], sems.at[i]
+        )
+        for i in range(PIECES)
+    ]
+    for copy in copies:
+        copy.start()
     scaled = scaled_ref[...].reshape(B, LANES)
-    out_ref[...] = jnp.dot(kernel_ref[...], scaled, preferred_element_type=F32).astype(BF)
+    for i, copy in enumerate(copies):
+        copy.wait()
+        rows = slice(i * ROWS, (i + 1) * ROWS)
+        out_ref[rows] = jnp.dot(held[rows], scaled, preferred_element_type=F32).astype(BF)
 
 
 def second_product(scaled, kernel):
     return pl.pallas_call(
         second_kernel,
+        in_specs=[
+            pl.BlockSpec(memory_space=pltpu.VMEM),
+            pl.BlockSpec(memory_space=pltpu.HBM),
+        ],
         out_shape=jax.ShapeDtypeStruct((A, LANES), BF),
-        compiler_params=PARAMS,
+        scratch_shapes=[pltpu.VMEM((A, B), BF), pltpu.SemaphoreType.DMA((PIECES,))],
+        compiler_params=pltpu.CompilerParams(vmem_limit_bytes=60 * 1024 * 1024),
         cost_estimate=pl.CostEstimate(
             flops=2 * A * B * LANES, bytes_accessed=5 << 20, transcendentals=0
         ),
@@ -113,23 +160,19 @@
 
 def per_device(embeddings, prior_scores, seed_labels, tile_pattern):
     z, xl = lax.axis_index("z"), lax.axis_index("xl")
-    halves = [embeddings[:, :LANES], embeddings[:, LANES:]]
-
-    flags = jnp.repeat(tile_pattern[:, 0].astype(BF), LANES // 2)
-    flags = jnp.broadcast_to(flags[None, :], (8, LANES))
+    loads, stacked = make_loads(embeddings, prior_scores)
+
+    flags = jnp.repeat(tile_pattern.astype(BF), 4, axis=0)
+    flags = jnp.broadcast_to(flags, (8, LANES))
     other = lax.ppermute(flags, "xl", [(0, 1), (1, 0)])
     flags = [jnp.where(xl == 0, flags, other), jnp.where(xl == 0, other, flags)]
 
-    panel = spread_gather(jnp.concatenate(halves + [prior_scores], 0), PLANE, 32)
-
-    column = lax.all_gather(jnp.concatenate(halves + flags, 0), "z", axis=0)
-    kept = column[:, 2 * N :: 8, :: LANES // 2]
-    kept = lax.dynamic_index_in_dim(kept, z // 8, 1, False)
-    offset = jnp.where(kept > 0, -RATE, DROPPED).astype(F32).reshape(8, 2, 2)
-    offset = offset.transpose(2, 1, 0).reshape(2, 16)
-    offset = jnp.broadcast_to(offset[..., None], (2, 16, LANES))
-
-    kernel, sums = similarity(column, panel, offset)
+    flags, loads = lax.optimization_barrier((flags, loads))
+    panel = lax.all_to_all(loads, PLANE, 0, 0, tiled=True)
+
+    column = lax.all_gather(jnp.concatenate([stacked] + flags, 0), "z", axis=0)
+    half = (z // 8).astype(jnp.int32).reshape(1)
+    kernel, sums = similarity(half, column, panel)
     parts = spread_gather(sums, PLANE, 32)
     part, inv = first_product(parts, panel, kernel)
     inv_own = lax.dynamic_index_in_dim(inv.reshape(32, N), lax.axis_index(PLANE), 0, False)[:, None]

time: 159 us -> 144 us (0.906)
  waiting for transfers between devices: 34.2 us -> 18.2 us
  Pallas kernels: 5.41 us -> 10.9 us
  local copies, waits for them, and re-layouts: 5.24 us -> 1.85 us
    ppermute x1, waiting for transfers between devices: 15.9 us -> 0.01 us  [per_device(): other = lax.ppermute(flags, 'xl', [(0, 1), (1, 0)])]
    pallas_call x2 -> x3, Pallas kernels: 3.16 us -> 8.61 us  [the longest x1 5.18 us: second_product(): pl.pallas_call(second_kernel, in_specs=[pl.BlockSpec(memory_space=pltpu.V...]
  transfers between devices with their start and end apart: 3 -> 3, of which waited for: 2 -> 1; matrix products, arithmetic and copies ran while one was open for 0% -> 0% of each run, Pallas kernels for 0% -> 1%
where the time goes in v5:
time: 144 us
  blocking collectives  91.7 us (64%)
  starting transfers between devices  19.3 us (13%)
  waiting for transfers between devices  18.2 us (13%)
  Pallas kernels  10.9 us (8%)
  local copies, waits for them, and re-layouts  1.85 us (1%)
  other arithmetic  1.62 us (1%)
    all_gather x1, blocking collectives, per_device(): column = lax.all_gather(jnp.concatenate([stacked] + flags, 0), 'z', axis=0)  36.5 us
    all_to_all x2, blocking collectives, spread_gather(): return lax.all_to_all(copies, axes, 0, 0, tiled=True)  28.2 us
    all_to_all x1, blocking collectives, per_device(): part = lax.all_to_all(part.reshape(16, N, LANES), 'z', 0, 0, tiled=True)  24.6 us
    all_to_all x1, waiting for transfers between devices, per_device(): part = lax.all_to_all(part.reshape(16, N, LANES), 'z', 0, 0, tiled=True)  18.2 us
    all_to_all x1, starting transfers between devices, per_device(): part = lax.all_to_all(part.reshape(16, N, LANES), 'z', 0, 0, tiled=True)  8.93 us
    all_to_all x1, starting transfers between devices, per_device(): panel = lax.all_to_all(loads, PLANE, 0, 0, tiled=True)  7.03 us
    pallas_call x1, Pallas kernels, second_product(): pl.pallas_call(second_kernel, in_specs=[pl.BlockSpec(memory_space=pltpu.V...  5.18 us
    ppermute x1, starting transfers between devices, per_device(): other = lax.ppermute(flags, 'xl', [(0, 1), (1, 0)])  3.39 us
  transfers between devices with their start and end apart: 3, of which 1 were waited for; matrix products, arithmetic and copies ran while one was open for 0% of the time, Pallas kernels for 1%

profile of v5, /device:TPU:32, one launch (start us, length us, event | category | flops | bytes accessed | tf_op | source)
XLA Modules:
  0.0 143.7 jit_solution(17710313070648114187)
XLA Ops:
  0.0 0.7 convert_bitcast_fusion
  0.7 0.1 broadcast_in_dim.12
  0.7 0.1 broadcast_in_dim.13
  0.8 0.1 broadcast_in_dim.14
  0.9 3.4 %collective-permute-start = (bf16[8,128]{1,0:T(8,128)(2,1)S(1)}, bf16[8,128]{1,0:T(8,128)(2,1)S(1)}, u32[]{:S(2)}, u32[]{:S(2)}) collective-permute-start(bf16[8,128]{1,0:T(8,128)(2,1)S(1)} %broadcast_in_dim.14), channel_id=1, source_target_pairs={{0,1},{1,0},{2,3},{3,2},{4,5},{5,4},{6,7},{7,6},{8,9},{9,8},{10,11... | collective-permute-start | bytes 6152 | tf_op jit(solution)/shard_map/ppermute | solution.py:167
  4.3 0.0 copy-start.1
  4.3 0.7 copy-done.1
  5.1 0.0 copy-start.2
  5.1 0.7 copy-done.2
  5.8 1.5 %make_loads.1 = (bf16[32,192,128]{2,1,0:T(8,128)(2,1)}, bf16[128,128]{1,0:T(8,128)(2,1)S(1)}) custom-call(bf16[64,256]{1,0:T(8,128)(2,1)S(1)} %copy-done.1, bf16[64,128]{1,0:T(8,128)(2,1)S(1)} %copy-done.2), custom_call_target="tpu_custom_call" | custom-call | bytes 4194304 | tf_op jit(solution)/shard_map/make_loads/pallas_call | solution.py:42
  7.3 0.0 collective-permute-done
  7.3 0.1 broadcast_select_fusion
  7.4 7.0 %all-to-all-start = ((bf16[32,192,128]{2,1,0:T(8,128)(2,1)}), bf16[32,192,128]{2,1,0:T(8,128)(2,1)S(1)}, u32[]{:S(2)}, u32[]{:S(2)}) async-start(bf16[32,192,128]{2,1,0:T(8,128)(2,1)} %get-tuple-element.18), calls=%async_computation | async-start | bytes 3145728 | tf_op jit(solution)/shard_map/all_to_all | solution.py:171
  14.4 36.5 %all-gather = bf16[2304,128]{1,0:T(8,128)(2,1)S(1)} all-gather(bf16[144,128]{1,0:T(8,128)(2,1)S(1)} %pad_maximum_fusion), channel_id=2, replica_groups=mesh['xh'=2,'y'=4,'core'=2,'z'=16,'xl'=2] {'z'}, dimensions={0}, use_global_device_ids=true | all-gather | bytes 626688 | tf_op jit(solution)/shard_map/all_gather | solution.py:173
  51.0 0.0 all-to-all-done.panel_ref
  51.0 1.9 %similarity.1 = (bf16[1024,2048]{1,0:T(8,128)(2,1)S(1)}, f32[16,128]{1,0:T(8,128)S(1)}) custom-call(s32[1]{0:T(128)} %bitcast.half_ref, bf16[16,144,128]{2,1,0:T(8,128)(2,1)S(1)} %bitcast.10, bf16[32,192,128]{2,1,0:T(8,128)(2,1)S(1)} %all-to-all-done.panel_ref), custom_call_target="tpu_custom_call" | custom-call | flops 1073741824 | bytes 4194304 | tf_op jit(solution)/shard_map/similarity/pallas_call | solution.py:85
  52.9 0.0 copy-start
  53.0 16.5 %all_to_all.25.parts_ref = f32[32,16,128]{2,1,0:T(8,128)S(1)} all-to-all(f32[32,16,128]{2,1,0:T(8,128)S(1)} %broadcast_in_dim.30), channel_id=1, replica_groups=mesh['xh'=2,'y'=4,'core'=2,'z'=16,'xl'=2] {'core','xh','y','xl'}, dimensions={0} | all-to-all | bytes 524288 | tf_op jit(solution)/shard_map/all_to_all | solution.py:30
  69.4 0.0 copy-start.3
  69.4 2.3 %first_product.1 = (bf16[1024,128]{1,0:T(8,128)(2,1)}, f32[16,128]{1,0:T(8,128)S(1)}) custom-call(f32[32,16,128]{2,1,0:T(8,128)S(1)} %all_to_all.25.parts_ref, bf16[32,192,128]{2,1,0:T(8,128)(2,1)S(1)} %all-to-all-done.panel_ref, bf16[1024,2048]{1,0:T(8,128)(2,1)S(1)} %get-tuple-element.20.kernel_ref), custom_call_target="tpu_custom_call" | custom-call | flops 536870912 | bytes 5242880 | tf_op jit(solution)/shard_map/first_product/pallas_call | solution.py:110
  71.7 0.0 copy-done
  71.7 8.9 %all-to-all-start.2 = ((bf16[16,64,128]{2,1,0:T(8,128)(2,1)}), bf16[16,64,128]{2,1,0:T(8,128)(2,1)S(1)}, u32[]{:S(2)}, u32[]{:S(2)}) async-start(bf16[16,64,128]{2,1,0:T(8,128)(2,1)} %bitcast.4), calls=%async_computation.2 | async-start | bytes 524288 | tf_op jit(solution)/shard_map/all_to_all | solution.py:182
  80.6 0.1 reshape.77
  80.7 18.2 %all-to-all-done.2 = bf16[16,64,128]{2,1,0:T(8,128)(2,1)S(1)} async-done(((bf16[16,64,128]{2,1,0:T(8,128)(2,1)}), bf16[16,64,128]{2,1,0:T(8,128)(2,1)S(1)}, u32[]{:S(2)}, u32[]{:S(2)}) %all-to-all-start.2) | async-done | bytes 262176 | tf_op jit(solution)/shard_map/all_to_all | solution.py:182
  99.0 0.0 copy-done.3
  99.0 0.1 fusion.1
  99.1 11.8 %all_to_all.26 = bf16[16,64,128]{2,1,0:T(8,128)(2,1)S(1)} all-to-all(bf16[16,64,128]{2,1,0:T(8,128)(2,1)S(1)} %broadcast_in_dim.32), channel_id=1, replica_groups=mesh['xh'=2,'y'=4,'core'=2,'z'=16,'xl'=2] {'xh','y','xl'}, dimensions={0} | all-to-all | bytes 524288 | tf_op jit(solution)/shard_map/all_to_all | solution.py:30
  110.9 2.3 %all-gather.1 = bf16[32,64,128]{2,1,0:T(8,128)(2,1)} all-gather(bf16[16,64,128]{2,1,0:T(8,128)(2,1)S(1)} %all_to_all.26), channel_id=3, replica_groups=mesh['xh'=2,'y'=4,'core'=2,'z'=16,'xl'=2] {'core'}, dimensions={0}, use_global_device_ids=true | all-gather | bytes 786432 | tf_op jit(solution)/shard_map/all_gather | solution.py:187
  113.2 5.2 %second_product.1 = bf16[1024,128]{1,0:T(8,128)(2,1)} custom-call(bf16[2,16,64,128]{3,2,1,0:T(8,128)(2,1)} %bitcast.11, bf16[1024,2048]{1,0:T(8,128)(2,1)} %copy-done), custom_call_target="tpu_custom_call" | custom-call | flops 536870912 | bytes 5242880 | tf_op jit(solution)/shard_map/second_product/pallas_call | solution.py:145
  118.4 24.6 %all_to_all.27 = bf16[16,64,128]{2,1,0:T(8,128)(2,1)S(1)} all-to-all(bf16[16,64,128]{2,1,0:T(8,128)(2,1)} %bitcast.12), channel_id=1, replica_groups=mesh['xh'=2,'y'=4,'core'=2,'z'=16,'xl'=2] {'z'}, dimensions={0} | all-to-all | bytes 524288 | tf_op jit(solution)/shard_map/all_to_all | solution.py:189
  143.0 0.7 select_add_fusion
  (6 shorter events, 0.2 us)
Async XLA Ops:
  0.9 6.4 %collective-permute-start = (bf16[8,128]{1,0:T(8,128)(2,1)S(1)}, bf16[8,128]{1,0:T(8,128)(2,1)S(1)}, u32[]{:S(2)}, u32[]{:S(2)}) collective-permute-start(bf16[8,128]{1,0:T(8,128)(2,1)S(1)} %broadcast_in_dim.14), channel_id=1, source_target_pairs={{0,1},{1,0},{2,3},{3,2},{4,5},{5,4},{6,7},{7,6},{8,9},{9,8},{10,11... | collective-permute-start | bytes 6152 | tf_op jit(solution)/shard_map/ppermute | solution.py:167
  4.3 0.8 copy-start.1
  5.1 0.7 copy-start.2
  7.4 43.6 %all-to-all-start = ((bf16[32,192,128]{2,1,0:T(8,128)(2,1)}), bf16[32,192,128]{2,1,0:T(8,128)(2,1)S(1)}, u32[]{:S(2)}, u32[]{:S(2)}) async-start(bf16[32,192,128]{2,1,0:T(8,128)(2,1)} %get-tuple-element.18), calls=%async_computation | async-start | bytes 3145728 | tf_op jit(solution)/shard_map/all_to_all | solution.py:171
  52.9 18.8 %copy-start = (bf16[1024,2048]{1,0:T(8,128)(2,1)}, bf16[1024,2048]{1,0:T(8,128)(2,1)S(1)}, u32[]{:S(2)}) copy-start(bf16[1024,2048]{1,0:T(8,128)(2,1)S(1)} %get-tuple-element.20.kernel_ref) | copy-start | bytes 12582916
  69.4 29.6 %copy-start.3 = (s32[64]{0:T(128)S(1)}, s32[64]{0:T(128)}, u32[]{:S(2)}) copy-start(s32[64]{0:T(128)} %param.6) | copy-start | bytes 772
  71.7 27.3 %all-to-all-start.2 = ((bf16[16,64,128]{2,1,0:T(8,128)(2,1)}), bf16[16,64,128]{2,1,0:T(8,128)(2,1)S(1)}, u32[]{:S(2)}, u32[]{:S(2)}) async-start(bf16[16,64,128]{2,1,0:T(8,128)(2,1)} %bitcast.4), calls=%async_computation.2 | async-start | bytes 524288 | tf_op jit(solution)/shard_map/all_to_all | solution.py:182

commit v6 on v5

v6 whole, which is shorter than its diff:
```python
import jax
import jax.numpy as jnp
from jax import lax
from jax.experimental import pallas as pl
from jax.experimental.pallas import tpu as pltpu
from jax.sharding import Mesh, PartitionSpec as P

KERNEL_SPREAD = 0.05
PROPAGATE_WEIGHT = 0.9
SEED_WEIGHT = 0.1
RATE = 1.4426950408889634 / KERNEL_SPREAD
DROPPED = -1.0e30

AXES = ("xh", "y", "core", "z", "xl")
SIZES = (2, 4, 2, 16, 2)
ROW = ("xh", "y", "core")
COL = ("z", "xl")
LANES = 128
N = 64
A = 16 * N
B = 32 * N
PLANE = ("core", "xh", "y", "xl")
PIECES = 4
DEPTH = B // PIECES
BF = jnp.bfloat16
F32 = jnp.float32
PARAMS = pltpu.CompilerParams(vmem_limit_bytes=24 * 1024 * 1024)


def spread_gather(x, axes, count):
    copies = jnp.broadcast_to(x[None], (count,) + x.shape)
    return lax.all_to_all(copies, axes, 0, 0, tiled=True)


def load_kernel(emb_ref, copies_ref, stacked_ref):
    emb = jnp.concatenate([emb_ref[:, :LANES], emb_ref[:, LANES:]], 0)
    stacked_ref[...] = emb
    for i in range(32):
        copies_ref[i] = emb


def make_loads(embeddings):
    return pl.pallas_call(
        load_kernel,
        out_shape=(
            jax.ShapeDtypeStruct((32, 2 * N, LANES), BF),
            jax.ShapeDtypeStruct((2 * N, LANES), BF),
        ),
        compiler_params=PARAMS,
        cost_estimate=pl.CostEstimate(flops=0, bytes_accessed=4 << 20, transcendentals=0),
        name="make_loads",
    )(embeddings)


def rows_of(ref, i):
    lo = ref[4 * i : 4 * i + 4, :N, :].reshape(4 * N, LANES)
    hi = ref[4 * i : 4 * i + 4, N : 2 * N, :].reshape(4 * N, LANES)
    return jnp.concatenate([lo, hi], 1)


def weigh(left, right):
    return lax.dot_general(left, right, (((1,), (1,)), ((), ())), preferred_element_type=F32) * RATE


def mask_offsets(half_ref, column_ref):
    offsets = []
    for b in range(16):
        flags = column_ref[(b % 8) * 2 + b // 8, 3 * N :, :].astype(F32)
        flags = jnp.where(half_ref[0] == 0, flags[:8], flags[8:])
        offsets.append(jnp.where(flags > 0.5, -RATE, DROPPED))
    return offsets


def first_block_kernel(half_ref, column_ref, panel_ref, kernel_ref, sums_ref):
    offsets = mask_offsets(half_ref, column_ref)
    for j in range(4):
        right = rows_of(column_ref, j)
        row = slice(4 * (j // 2), 4 * (j // 2) + 1)
        sums = jnp.zeros((1, 4 * N), F32)
        for i in range(8):
            weights = weigh(rows_of(panel_ref, i), right)
            for k in range(2):
                offset = offsets[2 * i + k][row]
                offset = jnp.concatenate([offset, offset], 1)
                tile = jnp.exp2(weights[2 * N * k : 2 * N * (k + 1)] + offset).astype(BF)
                top = 4 * N * i + 2 * N * k
                kernel_ref[top : top + 2 * N, 4 * N * j : 4 * N * (j + 1)] = tile
                sums = sums + jnp.sum(tile.astype(F32), axis=0, keepdims=True)
        sums_ref[2 * j : 2 * j + 1, :] = sums[:, :LANES]
        sums_ref[2 * j + 1 : 2 * j + 2, :] = sums[:, LANES:]


def second_block_kernel(half_ref, column_ref, panel_ref, *kernel_refs):
    offsets = mask_offsets(half_ref, column_ref)
    for j in range(8):
        right = rows_of(panel_ref, j)
        for i in range(4):
            row = slice(4 * (i // 2), 4 * (i // 2) + 1)
            offset = jnp.concatenate([offsets[2 * j][row], offsets[2 * j + 1][row]], 1)
            tile = jnp.exp2(weigh(rows_of(column_ref, i), right) + offset).astype(BF)
            at = 4 * N * j % DEPTH
            kernel_refs[4 * N * j // DEPTH][4 * N * i : 4 * N * (i + 1), at : at + 4 * N] = tile


def make_block(body, out_shape, name, half, column, panel):
    vmem = pl.BlockSpec(memory_space=pltpu.VMEM)
    return pl.pallas_call(
        body,
        in_specs=[pl.BlockSpec(memory_space=pltpu.SMEM), vmem, vmem],
        out_shape=out_shape,
        compiler_params=PARAMS,
        cost_estimate=pl.CostEstimate(
            flops=2 * A * B * 256, bytes_accessed=4 << 20, transcendentals=A * B
        ),
        name=name,
    )(half, column, panel)


def first_kernel(parts_ref, column_ref, kernel_ref, out_ref, inv_ref):
    inv = 1.0 / jnp.sqrt(jnp.sum(parts_ref[...], axis=0))
    inv_ref[...] = inv
    turned = inv.T
    scaled = []
    for k in range(8):
        prior = column_ref[2 * k : 2 * k + 2, 2 * N : 3 * N, :].reshape(2 * N, LANES).astype(F32)
        scaled.append((turned[:, k : k + 1] * prior).astype(BF))
    scaled = jnp.concatenate(scaled, 0)
    out_ref[...] = jnp.dot(kernel_ref[...], scaled, preferred_element_type=F32).astype(BF)


def first_product(parts, column, kernel):
    return pl.pallas_call(
        first_kernel,
        out_shape=(
            jax.ShapeDtypeStruct((B, LANES), BF),
            jax.ShapeDtypeStruct((8, LANES), F32),
        ),
        compiler_params=PARAMS,
        cost_estimate=pl.CostEstimate(
            flops=2 * A * B * LANES, bytes_accessed=5 << 20, transcendentals=0
        ),
        name="first_product",
    )(parts, column, kernel)


def second_kernel(scaled_ref, *refs):
    kernel_refs, out_ref = refs[:PIECES], refs[PIECES]
    shards = DEPTH // N
    total = None
    for i, kernel_ref in enumerate(kernel_refs):
        first = i * shards
        scaled = scaled_ref[first // 16, first % 16 : first % 16 + shards].reshape(DEPTH, LANES)
        part = jnp.dot(kernel_ref[...], scaled, preferred_element_type=F32)
        total = part if total is None else total + part
    out_ref[...] = total.astype(BF)


def second_product(scaled, blocks):
    return pl.pallas_call(
        second_kernel,
        out_shape=jax.ShapeDtypeStruct((A, LANES), BF),
        compiler_params=PARAMS,
        cost_estimate=pl.CostEstimate(
            flops=2 * A * B * LANES, bytes_accessed=5 << 20, transcendentals=0
        ),
        name="second_product",
    )(scaled, *blocks)


def per_device(embeddings, prior_scores, seed_labels, tile_pattern):
    z, xl = lax.axis_index("z"), lax.axis_index("xl")
    half = (z // 8).astype(jnp.int32).reshape(1)
    loads, stacked = make_loads(embeddings)

    flags = jnp.repeat(tile_pattern.astype(BF), 4, axis=0)
    flags = jnp.broadcast_to(flags, (8, LANES))
    other = lax.ppermute(flags, "xl", [(0, 1), (1, 0)])
    flags = [jnp.where(xl == 0, flags, other), jnp.where(xl == 0, other, flags)]

    flags, loads = lax.optimization_barrier((flags, loads))
    panel = lax.all_to_all(loads, PLANE, 0, 0, tiled=True)

    column = lax.all_gather(jnp.concatenate([stacked, prior_scores] + flags, 0), "z", axis=0)

    block_ba, sums = make_block(
        first_block_kernel,
        (jax.ShapeDtypeStruct((B, A), BF), jax.ShapeDtypeStruct((8, LANES), F32)),
        "block_ba",
        half,
        column,
        panel,
    )
    parts = spread_gather(sums, "z", 16)
    part, inv = first_product(parts, column, block_ba)
    inv_own = lax.dynamic_index_in_dim(inv.reshape(16, N), z, 0, False)[:, None]
    classes_iota = jnp.arange(LANES, dtype=jnp.int32)
    seeds = SEED_WEIGHT * (seed_labels[:, None] == classes_iota[None, :]).astype(F32)

    part = lax.all_to_all(part.reshape(32, N, LANES), PLANE, 0, 0, tiled=True)
    product = jnp.sum(part.astype(F32), axis=0)
    scores = PROPAGATE_WEIGHT * inv_own * product + seeds

    scaled = (inv_own * scores).astype(BF)
    scaled, column = lax.optimization_barrier((scaled, column))
    scaled = spread_gather(scaled, PLANE[1:], 16)
    piece = jax.ShapeDtypeStruct((A, DEPTH), BF)
    block_ab = make_block(second_block_kernel, (piece,) * PIECES, "block_ab", half, column, panel)
    scaled = lax.all_gather(scaled, "core", axis=0)
    part = second_product(scaled, block_ab)
    part = lax.all_to_all(part.reshape(16, N, LANES), "z", 0, 0, tiled=True)
    product = jnp.sum(part.astype(F32), axis=0)
    return PROPAGATE_WEIGHT * inv_own * product + seeds


def solution(mesh):
    return jax.shard_map(
        per_device,
        mesh=Mesh(mesh.devices.reshape(SIZES), AXES),
        in_specs=(P(AXES, None), P(AXES, None), P(AXES), P(ROW, COL)),
        out_specs=P(AXES, None),
        check_vma=False,
    )
```

time: 144 us -> 140 us (0.972)
  blocking collectives: 91.7 us -> 83.2 us
  local copies, waits for them, and re-layouts: 1.85 us -> 7.46 us
  Pallas kernels: 10.9 us -> 8.16 us
  starting transfers between devices: 19.3 us -> 22 us
  waiting for transfers between devices: 18.2 us -> 15.7 us
    all_to_all x2 -> x1, blocking collectives: 28.2 us -> 20.5 us  [spread_gather(): return lax.all_to_all(copies, axes, 0, 0, tiled=True)]
    unnamed x8 -> x16, local copies, waits for them, and re-layouts: 1.48 us -> 6.39 us
    pallas_call x4 -> x5, Pallas kernels: 10.9 us -> 8.16 us  [the longest x2 3.33 us: make_block(): pl.pallas_call(body, in_specs=[pl.BlockSpec(memory_space=pltpu.SMEM), vme...]
    all_to_all x1 -> x2, waiting for transfers between devices: 18.2 us -> 15.6 us  [the longest x1 11.5 us: per_device(): part = lax.all_to_all(part.reshape(32, N, LANES), PLANE, 0, 0, tiled=True)]
    all_to_all x1 -> x2, starting transfers between devices: 8.93 us -> 11.3 us  [the longest x1 7.23 us: per_device(): part = lax.all_to_all(part.reshape(32, N, LANES), PLANE, 0, 0, tiled=True)]
    all_to_all x1, blocking collectives: 24.6 us -> 22.3 us  [per_device(): part = lax.all_to_all(part.reshape(16, N, LANES), 'z', 0, 0, tiled=True)]
    all_gather x1, blocking collectives: 36.5 us -> 38.2 us  [per_device(): lax.all_gather(jnp.concatenate([stacked, prior_scores] + flags, 0), 'z',...]
  transfers between devices with their start and end apart: 3 -> 4, of which waited for: 1 -> 3; matrix products, arithmetic and copies ran while one was open for 0% -> 1% of each run, Pallas kernels for 1% -> 2%
where the time goes in v6:
time: 140 us; the launch traced here: 139 us
  blocking collectives  83.2 us (59%)
  starting transfers between devices  22 us (16%)
  waiting for transfers between devices  15.7 us (11%)
  Pallas kernels  8.16 us (6%)
  local copies, waits for them, and re-layouts  7.46 us (5%)
  other arithmetic  2.38 us (2%)
    all_gather x1, blocking collectives, per_device(): lax.all_gather(jnp.concatenate([stacked, prior_scores] + flags, 0), 'z',...  38.2 us
    all_to_all x1, blocking collectives, per_device(): part = lax.all_to_all(part.reshape(16, N, LANES), 'z', 0, 0, tiled=True)  22.3 us
    all_to_all x1, blocking collectives, spread_gather(): return lax.all_to_all(copies, axes, 0, 0, tiled=True)  20.5 us
    all_to_all x1, waiting for transfers between devices, per_device(): part = lax.all_to_all(part.reshape(32, N, LANES), PLANE, 0, 0, tiled=True)  11.5 us
    all_to_all x1, starting transfers between devices, per_device(): panel = lax.all_to_all(loads, PLANE, 0, 0, tiled=True)  7.32 us
    all_to_all x1, starting transfers between devices, per_device(): part = lax.all_to_all(part.reshape(32, N, LANES), PLANE, 0, 0, tiled=True)  7.23 us
    unnamed x16, local copies, waits for them, and re-layouts  6.39 us
    all_to_all x1, waiting for transfers between devices, spread_gather(): return lax.all_to_all(copies, axes, 0, 0, tiled=True)  4.15 us
  transfers between devices with their start and end apart: 4, of which 3 were waited for; matrix products, arithmetic and copies ran while one was open for 1% of the time, Pallas kernels for 2%

profile of v6, /device:TPU:32, one launch (start us, length us, event | category | flops | bytes accessed | tf_op | source)
XLA Modules:
  0.0 139.0 jit_solution(2908702835878715856)
XLA Ops:
  0.0 0.7 convert_bitcast_fusion
  0.7 0.1 broadcast_in_dim.12
  0.7 0.1 broadcast_in_dim.13
  0.8 0.1 broadcast_in_dim.14
  0.9 3.4 %collective-permute-start = (bf16[8,128]{1,0:T(8,128)(2,1)S(1)}, bf16[8,128]{1,0:T(8,128)(2,1)S(1)}, u32[]{:S(2)}, u32[]{:S(2)}) collective-permute-start(bf16[8,128]{1,0:T(8,128)(2,1)S(1)} %broadcast_in_dim.14), channel_id=1, source_target_pairs={{0,1},{1,0},{2,3},{3,2},{4,5},{5,4},{6,7},{7,6},{8,9},{9,8},{10,11... | collective-permute-start | bytes 6152 | tf_op jit(solution)/shard_map/ppermute | solution.py:177
  4.3 0.0 copy-start.6
  4.3 0.7 copy-done.6
  5.1 1.2 make_loads.1
  6.3 0.1 collective-permute-done
  6.4 0.1 broadcast_select_fusion
  6.4 7.3 %all-to-all-start = ((bf16[32,128,128]{2,1,0:T(8,128)(2,1)}), bf16[32,128,128]{2,1,0:T(8,128)(2,1)S(1)}, u32[]{:S(2)}, u32[]{:S(2)}) async-start(bf16[32,128,128]{2,1,0:T(8,128)(2,1)} %get-tuple-element.24), calls=%async_computation | async-start | bytes 2097152 | tf_op jit(solution)/shard_map/all_to_all | solution.py:181
  13.8 0.7 pad_maximum_fusion
  14.5 38.2 %all-gather = bf16[3328,128]{1,0:T(8,128)(2,1)S(1)} all-gather(bf16[208,128]{1,0:T(8,128)(2,1)S(1)} %pad_maximum_fusion), channel_id=2, replica_groups=mesh['xh'=2,'y'=4,'core'=2,'z'=16,'xl'=2] {'z'}, dimensions={0}, use_global_device_ids=true | all-gather | bytes 905216 | tf_op jit(solution)/shard_map/all_gather | solution.py:183
  52.7 0.0 all-to-all-done.panel_ref
  52.7 0.0 copy-start.4
  52.7 2.0 %block_ba.1 = (bf16[2048,1024]{1,0:T(8,128)(2,1)S(1)}, f32[8,128]{1,0:T(8,128)S(1)}) custom-call(s32[1]{0:T(128)} %bitcast.half_ref, bf16[16,208,128]{2,1,0:T(8,128)(2,1)S(1)} %bitcast.10, bf16[32,128,128]{2,1,0:T(8,128)(2,1)S(1)} %all-to-all-done.panel_ref), custom_call_target="tpu_custom_call" | custom-call | flops 1073741824 | bytes 4194304 | tf_op jit(solution)/shard_map/block_ba/pallas_call | solution.py:107
  54.7 0.0 copy-start.7
  54.7 20.5 %all_to_all.25.parts_ref = f32[16,8,128]{2,1,0:T(8,128)S(1)} all-to-all(f32[16,8,128]{2,1,0:T(8,128)S(1)} %broadcast_in_dim.30), channel_id=1, replica_groups=mesh['xh'=2,'y'=4,'core'=2,'z'=16,'xl'=2] {'z'}, dimensions={0} | all-to-all | bytes 131072 | tf_op jit(solution)/shard_map/all_to_all | solution.py:32
  75.2 2.4 %first_product.1 = (bf16[2048,128]{1,0:T(8,128)(2,1)}, f32[8,128]{1,0:T(8,128)S(1)}) custom-call(f32[16,8,128]{2,1,0:T(8,128)S(1)} %all_to_all.25.parts_ref, bf16[16,208,128]{2,1,0:T(8,128)(2,1)S(1)} %bitcast.11, bf16[2048,1024]{1,0:T(8,128)(2,1)S(1)} %get-tuple-element.26.kernel_ref), custom_call_target="tpu_custom_call" | custom-call | flops 536870912 | bytes 5242880 | tf_op jit(solution)/shard_map/first_product/pallas_call | solution.py:132
  77.6 0.0 copy-done.4
  77.6 7.2 %all-to-all-start.2 = ((bf16[32,64,128]{2,1,0:T(8,128)(2,1)}), bf16[32,64,128]{2,1,0:T(8,128)(2,1)S(1)}, u32[]{:S(2)}, u32[]{:S(2)}) async-start(bf16[32,64,128]{2,1,0:T(8,128)(2,1)} %bitcast.4), calls=%async_computation.2 | async-start | bytes 1048576 | tf_op jit(solution)/shard_map/all_to_all | solution.py:199
  84.8 0.1 reshape.30
  84.9 11.5 %all-to-all-done.2 = bf16[32,64,128]{2,1,0:T(8,128)(2,1)S(1)} async-done(((bf16[32,64,128]{2,1,0:T(8,128)(2,1)}), bf16[32,64,128]{2,1,0:T(8,128)(2,1)S(1)}, u32[]{:S(2)}, u32[]{:S(2)}) %all-to-all-start.2) | async-done | bytes 524320 | tf_op jit(solution)/shard_map/all_to_all | solution.py:199
  96.4 0.1 convert_reduce_fusion
  96.4 0.0 copy-done.7
  96.5 0.1 fusion.1
  96.6 0.8 broadcast_in_dim.32
  97.3 4.1 %all-to-all-start.3 = ((bf16[16,64,128]{2,1,0:T(8,128)(2,1)}), bf16[16,64,128]{2,1,0:T(8,128)(2,1)S(1)}, u32[]{:S(2)}, u32[]{:S(2)}) async-start(bf16[16,64,128]{2,1,0:T(8,128)(2,1)} %broadcast_in_dim.32), calls=%async_computation.3 | async-start | bytes 524288 | tf_op jit(solution)/shard_map/all_to_all | solution.py:32
  101.4 0.0 copy-start.5
  101.4 1.2 copy-done.5
  102.6 1.3 block_ab.1
  103.9 0.0 copy-start
  103.9 1.0 copy-done
  104.9 0.0 copy-start.2
  104.9 1.0 copy-done.2
  105.9 4.2 %all-to-all-done.3 = bf16[16,64,128]{2,1,0:T(8,128)(2,1)S(1)} async-done(((bf16[16,64,128]{2,1,0:T(8,128)(2,1)}), bf16[16,64,128]{2,1,0:T(8,128)(2,1)S(1)}, u32[]{:S(2)}, u32[]{:S(2)}) %all-to-all-start.3) | async-done | bytes 262176 | tf_op jit(solution)/shard_map/all_to_all | solution.py:32
  110.1 2.2 %all-gather.1 = bf16[32,64,128]{2,1,0:T(8,128)(2,1)S(1)} all-gather(bf16[16,64,128]{2,1,0:T(8,128)(2,1)S(1)} %all-to-all-done.3), channel_id=3, replica_groups=mesh['xh'=2,'y'=4,'core'=2,'z'=16,'xl'=2] {'core'}, dimensions={0}, use_global_device_ids=true | all-gather | bytes 786432 | tf_op jit(solution)/shard_map/all_gather | solution.py:208
  112.2 0.0 copy-start.1
  112.2 1.2 copy-done.1
  113.5 0.0 copy-start.3
  113.5 1.2 copy-done.3
  114.7 1.2 second_product.1
  115.9 22.3 %all_to_all.26 = bf16[16,64,128]{2,1,0:T(8,128)(2,1)S(1)} all-to-all(bf16[16,64,128]{2,1,0:T(8,128)(2,1)S(1)} %bitcast.14), channel_id=1, replica_groups=mesh['xh'=2,'y'=4,'core'=2,'z'=16,'xl'=2] {'z'}, dimensions={0} | all-to-all | bytes 524288 | tf_op jit(solution)/shard_map/all_to_all | solution.py:210
  138.3 0.7 select_add_fusion
  (3 shorter events, 0.1 us)
Async XLA Ops:
  0.9 5.5 %collective-permute-start = (bf16[8,128]{1,0:T(8,128)(2,1)S(1)}, bf16[8,128]{1,0:T(8,128)(2,1)S(1)}, u32[]{:S(2)}, u32[]{:S(2)}) collective-permute-start(bf16[8,128]{1,0:T(8,128)(2,1)S(1)} %broadcast_in_dim.14), channel_id=1, source_target_pairs={{0,1},{1,0},{2,3},{3,2},{4,5},{5,4},{6,7},{7,6},{8,9},{9,8},{10,11... | collective-permute-start | bytes 6152 | tf_op jit(solution)/shard_map/ppermute | solution.py:177
  4.3 0.8 copy-start.6
  6.4 46.3 %all-to-all-start = ((bf16[32,128,128]{2,1,0:T(8,128)(2,1)}), bf16[32,128,128]{2,1,0:T(8,128)(2,1)S(1)}, u32[]{:S(2)}, u32[]{:S(2)}) async-start(bf16[32,128,128]{2,1,0:T(8,128)(2,1)} %get-tuple-element.24), calls=%async_computation | async-start | bytes 2097152 | tf_op jit(solution)/shard_map/all_to_all | solution.py:181
  52.7 24.9 %copy-start.4 = (bf16[32,128,128]{2,1,0:T(8,128)(2,1)}, bf16[32,128,128]{2,1,0:T(8,128)(2,1)S(1)}, u32[]{:S(2)}) copy-start(bf16[32,128,128]{2,1,0:T(8,128)(2,1)S(1)} %all-to-all-done.panel_ref) | copy-start | bytes 3145732
  54.7 41.7 %copy-start.7 = (s32[64]{0:T(128)S(1)}, s32[64]{0:T(128)}, u32[]{:S(2)}) copy-start(s32[64]{0:T(128)} %param.6) | copy-start | bytes 772
  77.6 18.8 %all-to-all-start.2 = ((bf16[32,64,128]{2,1,0:T(8,128)(2,1)}), bf16[32,64,128]{2,1,0:T(8,128)(2,1)S(1)}, u32[]{:S(2)}, u32[]{:S(2)}) async-start(bf16[32,64,128]{2,1,0:T(8,128)(2,1)} %bitcast.4), calls=%async_computation.2 | async-start | bytes 1048576 | tf_op jit(solution)/shard_map/all_to_all | solution.py:199
  97.3 12.8 %all-to-all-start.3 = ((bf16[16,64,128]{2,1,0:T(8,128)(2,1)}), bf16[16,64,128]{2,1,0:T(8,128)(2,1)S(1)}, u32[]{:S(2)}, u32[]{:S(2)}) async-start(bf16[16,64,128]{2,1,0:T(8,128)(2,1)} %broadcast_in_dim.32), calls=%async_computation.3 | async-start | bytes 524288 | tf_op jit(solution)/shard_map/all_to_all | solution.py:32
  101.4 1.2 copy-start.5
  103.9 1.0 copy-start
  104.9 1.0 copy-start.2
  112.2 1.2 copy-start.1
  113.5 1.2 copy-start.3

commit v7 on v6

--- a/solution.py
+++ b/solution.py
@@ -20,8 +20,6 @@
 A = 16 * N
 B = 32 * N
 PLANE = ("core", "xh", "y", "xl")
-PIECES = 4
-DEPTH = B // PIECES
 BF = jnp.bfloat16
 F32 = jnp.float32
 PARAMS = pltpu.CompilerParams(vmem_limit_bytes=24 * 1024 * 1024)
@@ -32,24 +30,25 @@
     return lax.all_to_all(copies, axes, 0, 0, tiled=True)
 
 
-def load_kernel(emb_ref, copies_ref, stacked_ref):
+def load_kernel(emb_ref, prior_ref, copies_ref, stacked_ref):
     emb = jnp.concatenate([emb_ref[:, :LANES], emb_ref[:, LANES:]], 0)
-    stacked_ref[...] = emb
+    stacked_ref[: 2 * N] = emb
+    stacked_ref[2 * N :] = prior_ref[...]
     for i in range(32):
         copies_ref[i] = emb
 
 
-def make_loads(embeddings):
+def make_loads(embeddings, prior_scores):
     return pl.pallas_call(
         load_kernel,
         out_shape=(
             jax.ShapeDtypeStruct((32, 2 * N, LANES), BF),
-            jax.ShapeDtypeStruct((2 * N, LANES), BF),
+            jax.ShapeDtypeStruct((3 * N, LANES), BF),
         ),
         compiler_params=PARAMS,
         cost_estimate=pl.CostEstimate(flops=0, bytes_accessed=4 << 20, transcendentals=0),
         name="make_loads",
-    )(embeddings)
+    )(embeddings, prior_scores)
 
 
 def rows_of(ref, i):
@@ -90,29 +89,17 @@
         sums_ref[2 * j + 1 : 2 * j + 2, :] = sums[:, LANES:]
 
 
-def second_block_kernel(half_ref, column_ref, panel_ref, *kernel_refs):
-    offsets = mask_offsets(half_ref, column_ref)
-    for j in range(8):
-        right = rows_of(panel_ref, j)
-        for i in range(4):
-            row = slice(4 * (i // 2), 4 * (i // 2) + 1)
-            offset = jnp.concatenate([offsets[2 * j][row], offsets[2 * j + 1][row]], 1)
-            tile = jnp.exp2(weigh(rows_of(column_ref, i), right) + offset).astype(BF)
-            at = 4 * N * j % DEPTH
-            kernel_refs[4 * N * j // DEPTH][4 * N * i : 4 * N * (i + 1), at : at + 4 * N] = tile
-
-
-def make_block(body, out_shape, name, half, column, panel):
+def first_block(half, column, panel):
     vmem = pl.BlockSpec(memory_space=pltpu.VMEM)
     return pl.pallas_call(
-        body,
+        first_block_kernel,
         in_specs=[pl.BlockSpec(memory_space=pltpu.SMEM), vmem, vmem],
-        out_shape=out_shape,
+        out_shape=(jax.ShapeDtypeStruct((B, A), BF), jax.ShapeDtypeStruct((8, LANES), F32)),
         compiler_params=PARAMS,
         cost_estimate=pl.CostEstimate(
             flops=2 * A * B * 256, bytes_accessed=4 << 20, transcendentals=A * B
         ),
-        name=name,
+        name="first_block",
     )(half, column, panel)
 
 
@@ -143,34 +130,39 @@
     )(parts, column, kernel)
 
 
-def second_kernel(scaled_ref, *refs):
-    kernel_refs, out_ref = refs[:PIECES], refs[PIECES]
-    shards = DEPTH // N
-    total = None
-    for i, kernel_ref in enumerate(kernel_refs):
-        first = i * shards
-        scaled = scaled_ref[first // 16, first % 16 : first % 16 + shards].reshape(DEPTH, LANES)
-        part = jnp.dot(kernel_ref[...], scaled, preferred_element_type=F32)
-        total = part if total is None else total + part
-    out_ref[...] = total.astype(BF)
-
-
-def second_product(scaled, blocks):
+def second_kernel(half_ref, column_ref, panel_ref, scaled_ref, out_ref):
+    offsets = mask_offsets(half_ref, column_ref)
+    for i in range(4):
+        row = slice(4 * (i // 2), 4 * (i // 2) + 1)
+        left = rows_of(column_ref, i)
+        total = jnp.zeros((4 * N, LANES), F32)
+        for j in range(8):
+            offset = jnp.concatenate([offsets[2 * j][row], offsets[2 * j + 1][row]], 1)
+            tile = jnp.exp2(weigh(left, rows_of(panel_ref, j)) + offset).astype(BF)
+            at = 4 * j % 16
+            scaled = scaled_ref[j // 4, at : at + 4].reshape(4 * N, LANES)
+            total = total + jnp.dot(tile, scaled, preferred_element_type=F32)
+        out_ref[4 * N * i : 4 * N * (i + 1)] = total.astype(BF)
+
+
+def second_product(half, column, panel, scaled):
+    vmem = pl.BlockSpec(memory_space=pltpu.VMEM)
     return pl.pallas_call(
         second_kernel,
+        in_specs=[pl.BlockSpec(memory_space=pltpu.SMEM), vmem, vmem, vmem],
         out_shape=jax.ShapeDtypeStruct((A, LANES), BF),
         compiler_params=PARAMS,
         cost_estimate=pl.CostEstimate(
-            flops=2 * A * B * LANES, bytes_accessed=5 << 20, transcendentals=0
+            flops=2 * A * B * (256 + LANES), bytes_accessed=3 << 20, transcendentals=A * B
         ),
         name="second_product",
-    )(scaled, *blocks)
+    )(half, column, panel, scaled)
 
 
 def per_device(embeddings, prior_scores, seed_labels, tile_pattern):
     z, xl = lax.axis_index("z"), lax.axis_index("xl")
     half = (z // 8).astype(jnp.int32).reshape(1)
-    loads, stacked = make_loads(embeddings)
+    loads, stacked = make_loads(embeddings, prior_scores)
 
     flags = jnp.repeat(tile_pattern.astype(BF), 4, axis=0)
     flags = jnp.broadcast_to(flags, (8, LANES))
@@ -180,18 +172,11 @@
     flags, loads = lax.optimization_barrier((flags, loads))
     panel = lax.all_to_all(loads, PLANE, 0, 0, tiled=True)
 
-    column = lax.all_gather(jnp.concatenate([stacked, prior_scores] + flags, 0), "z", axis=0)
-
-    block_ba, sums = make_block(
-        first_block_kernel,
-        (jax.ShapeDtypeStruct((B, A), BF), jax.ShapeDtypeStruct((8, LANES), F32)),
-        "block_ba",
-        half,
-        column,
-        panel,
-    )
+    column = lax.all_gather(jnp.concatenate([stacked] + flags, 0), "z", axis=0)
+
+    block, sums = first_block(half, column, panel)
     parts = spread_gather(sums, "z", 16)
-    part, inv = first_product(parts, column, block_ba)
+    part, inv = first_product(parts, column, block)
     inv_own = lax.dynamic_index_in_dim(inv.reshape(16, N), z, 0, False)[:, None]
     classes_iota = jnp.arange(LANES, dtype=jnp.int32)
     seeds = SEED_WEIGHT * (seed_labels[:, None] == classes_iota[None, :]).astype(F32)
@@ -200,13 +185,9 @@
     product = jnp.sum(part.astype(F32), axis=0)
     scores = PROPAGATE_WEIGHT * inv_own * product + seeds
 
-    scaled = (inv_own * scores).astype(BF)
-    scaled, column = lax.optimization_barrier((scaled, column))
-    scaled = spread_gather(scaled, PLANE[1:], 16)
-    piece = jax.ShapeDtypeStruct((A, DEPTH), BF)
-    block_ab = make_block(second_block_kernel, (piece,) * PIECES, "block_ab", half, column, panel)
+    scaled = spread_gather((inv_own * scores).astype(BF), PLANE[1:], 16)
     scaled = lax.all_gather(scaled, "core", axis=0)
-    part = second_product(scaled, block_ab)
+    part = second_product(half, column, panel, scaled)
     part = lax.all_to_all(part.reshape(16, N, LANES), "z", 0, 0, tiled=True)
     product = jnp.sum(part.astype(F32), axis=0)
     return PROPAGATE_WEIGHT * inv_own * product + seeds

time: 140 us -> 138 us (0.986)
  blocking collectives: 83.2 us -> 95.6 us
  local copies, waits for them, and re-layouts: 7.46 us -> 1.83 us
  waiting for transfers between devices: 15.7 us -> 11.5 us
  starting transfers between devices: 22 us -> 18 us
    all_to_all x1 -> x2, blocking collectives: 20.5 us -> 32.9 us  [spread_gather(): return lax.all_to_all(copies, axes, 0, 0, tiled=True)]
    unnamed x16 -> x6, local copies, waits for them, and re-layouts: 6.39 us -> 1.48 us
    all_to_all x1 -> x0, waiting for transfers between devices: 4.15 us -> none  [spread_gather(): return lax.all_to_all(copies, axes, 0, 0, tiled=True)]
    all_to_all x1 -> x0, starting transfers between devices: 4.06 us -> none  [spread_gather(): return lax.all_to_all(copies, axes, 0, 0, tiled=True)]
    pallas_call x3 -> x2, Pallas kernels: 4.57 us -> 5.17 us  [the longest x1 3.17 us: second_product(): pl.pallas_call(second_kernel, in_specs=[pl.BlockSpec(memory_space=pltpu.S...]
  transfers between devices with their start and end apart: 4 -> 3, of which waited for: 3 -> 1; matrix products, arithmetic and copies ran while one was open for 1% -> 0% of each run, Pallas kernels for 2% -> 1%
where the time goes in v7:
time: 138 us; the launch traced here: 137 us
  blocking collectives  95.6 us (69%)
  starting transfers between devices  18 us (13%)
  waiting for transfers between devices  11.5 us (8%)
  Pallas kernels  8.7 us (6%)
  local copies, waits for them, and re-layouts  1.83 us (1%)
  other arithmetic  1.66 us (1%)
    all_gather x1, blocking collectives, per_device(): column = lax.all_gather(jnp.concatenate([stacked] + flags, 0), 'z', axis=0)  38.2 us
    all_to_all x2, blocking collectives, spread_gather(): return lax.all_to_all(copies, axes, 0, 0, tiled=True)  32.9 us
    all_to_all x1, blocking collectives, per_device(): part = lax.all_to_all(part.reshape(16, N, LANES), 'z', 0, 0, tiled=True)  22.3 us
    all_to_all x1, waiting for transfers between devices, per_device(): part = lax.all_to_all(part.reshape(32, N, LANES), PLANE, 0, 0, tiled=True)  11.5 us
    all_to_all x1, starting transfers between devices, per_device(): part = lax.all_to_all(part.reshape(32, N, LANES), PLANE, 0, 0, tiled=True)  7.59 us
    all_to_all x1, starting transfers between devices, per_device(): panel = lax.all_to_all(loads, PLANE, 0, 0, tiled=True)  7.03 us
    ppermute x1, starting transfers between devices, per_device(): other = lax.ppermute(flags, 'xl', [(0, 1), (1, 0)])  3.39 us
    pallas_call x1, Pallas kernels, second_product(): pl.pallas_call(second_kernel, in_specs=[pl.BlockSpec(memory_space=pltpu.S...  3.17 us
  transfers between devices with their start and end apart: 3, of which 1 were waited for; matrix products, arithmetic and copies ran while one was open for 0% of the time, Pallas kernels for 1%

profile of v7, /device:TPU:32, one launch (start us, length us, event | category | flops | bytes accessed | tf_op | source)
XLA Modules:
  0.0 137.4 jit_solution(9360704764930970261)
XLA Ops:
  0.0 0.7 convert_bitcast_fusion
  0.7 0.1 broadcast_in_dim.12
  0.7 0.1 broadcast_in_dim.13
  0.8 0.1 broadcast_in_dim.14
  0.9 3.4 %collective-permute-start = (bf16[8,128]{1,0:T(8,128)(2,1)S(1)}, bf16[8,128]{1,0:T(8,128)(2,1)S(1)}, u32[]{:S(2)}, u32[]{:S(2)}) collective-permute-start(bf16[8,128]{1,0:T(8,128)(2,1)S(1)} %broadcast_in_dim.14), channel_id=1, source_target_pairs={{0,1},{1,0},{2,3},{3,2},{4,5},{5,4},{6,7},{7,6},{8,9},{9,8},{10,11... | collective-permute-start | bytes 6152 | tf_op jit(solution)/shard_map/ppermute | solution.py:169
  4.3 0.0 copy-start
  4.3 0.7 copy-done
  5.1 0.0 copy-start.1
  5.1 0.7 copy-done.1
  5.8 1.2 make_loads.1
  7.0 0.0 collective-permute-done
  7.0 0.1 broadcast_select_fusion
  7.1 7.0 %all-to-all-start = ((bf16[32,128,128]{2,1,0:T(8,128)(2,1)}), bf16[32,128,128]{2,1,0:T(8,128)(2,1)S(1)}, u32[]{:S(2)}, u32[]{:S(2)}) async-start(bf16[32,128,128]{2,1,0:T(8,128)(2,1)} %get-tuple-element.18), calls=%async_computation | async-start | bytes 2097152 | tf_op jit(solution)/shard_map/all_to_all | solution.py:173
  14.1 38.2 %all-gather = bf16[3328,128]{1,0:T(8,128)(2,1)S(1)} all-gather(bf16[208,128]{1,0:T(8,128)(2,1)S(1)} %pad_maximum_fusion), channel_id=2, replica_groups=mesh['xh'=2,'y'=4,'core'=2,'z'=16,'xl'=2] {'z'}, dimensions={0}, use_global_device_ids=true | all-gather | bytes 905216 | tf_op jit(solution)/shard_map/all_gather | solution.py:175
  52.4 0.0 all-to-all-done.panel_ref
  52.4 2.0 %first_block.1 = (bf16[2048,1024]{1,0:T(8,128)(2,1)S(1)}, f32[8,128]{1,0:T(8,128)S(1)}) custom-call(s32[1]{0:T(128)} %bitcast.half_ref, bf16[16,208,128]{2,1,0:T(8,128)(2,1)S(1)} %bitcast.10, bf16[32,128,128]{2,1,0:T(8,128)(2,1)S(1)} %all-to-all-done.panel_ref), custom_call_target="tpu_custom_call" | custom-call | flops 1073741824 | bytes 4194304 | tf_op jit(solution)/shard_map/first_block/pallas_call | solution.py:94
  54.4 0.0 copy-start.2
  54.4 20.4 %all_to_all.25.parts_ref = f32[16,8,128]{2,1,0:T(8,128)S(1)} all-to-all(f32[16,8,128]{2,1,0:T(8,128)S(1)} %broadcast_in_dim.30), channel_id=1, replica_groups=mesh['xh'=2,'y'=4,'core'=2,'z'=16,'xl'=2] {'z'}, dimensions={0} | all-to-all | bytes 131072 | tf_op jit(solution)/shard_map/all_to_all | solution.py:30
  74.7 2.3 %first_product.1 = (bf16[2048,128]{1,0:T(8,128)(2,1)}, f32[8,128]{1,0:T(8,128)S(1)}) custom-call(f32[16,8,128]{2,1,0:T(8,128)S(1)} %all_to_all.25.parts_ref, bf16[16,208,128]{2,1,0:T(8,128)(2,1)S(1)} %bitcast.11, bf16[2048,1024]{1,0:T(8,128)(2,1)S(1)} %get-tuple-element.20.kernel_ref), custom_call_target="tpu_custom_call" | custom-call | flops 536870912 | bytes 5242880 | tf_op jit(solution)/shard_map/first_product/pallas_call | solution.py:119
  77.1 7.6 %all-to-all-start.2 = ((bf16[32,64,128]{2,1,0:T(8,128)(2,1)}), bf16[32,64,128]{2,1,0:T(8,128)(2,1)S(1)}, u32[]{:S(2)}, u32[]{:S(2)}) async-start(bf16[32,64,128]{2,1,0:T(8,128)(2,1)} %bitcast.4), calls=%async_computation.2 | async-start | bytes 1048576 | tf_op jit(solution)/shard_map/all_to_all | solution.py:184
  84.7 0.1 reshape.77
  84.7 11.5 %all-to-all-done.2 = bf16[32,64,128]{2,1,0:T(8,128)(2,1)S(1)} async-done(((bf16[32,64,128]{2,1,0:T(8,128)(2,1)}), bf16[32,64,128]{2,1,0:T(8,128)(2,1)S(1)}, u32[]{:S(2)}, u32[]{:S(2)}) %all-to-all-start.2) | async-done | bytes 524320 | tf_op jit(solution)/shard_map/all_to_all | solution.py:184
  96.2 0.1 convert_reduce_fusion
  96.3 0.0 copy-done.2
  96.3 0.1 fusion.1
  96.4 12.6 %all_to_all.26 = bf16[16,64,128]{2,1,0:T(8,128)(2,1)S(1)} all-to-all(bf16[16,64,128]{2,1,0:T(8,128)(2,1)S(1)} %broadcast_in_dim.32), channel_id=1, replica_groups=mesh['xh'=2,'y'=4,'core'=2,'z'=16,'xl'=2] {'xh','y','xl'}, dimensions={0} | all-to-all | bytes 524288 | tf_op jit(solution)/shard_map/all_to_all | solution.py:30
  109.0 2.2 %all-gather.1 = bf16[32,64,128]{2,1,0:T(8,128)(2,1)S(1)} all-gather(bf16[16,64,128]{2,1,0:T(8,128)(2,1)S(1)} %all_to_all.26), channel_id=3, replica_groups=mesh['xh'=2,'y'=4,'core'=2,'z'=16,'xl'=2] {'core'}, dimensions={0}, use_global_device_ids=true | all-gather | bytes 786432 | tf_op jit(solution)/shard_map/all_gather | solution.py:189
  111.2 3.2 %second_product.1 = bf16[1024,128]{1,0:T(8,128)(2,1)S(1)} custom-call(s32[1]{0:T(128)} %bitcast.half_ref, bf16[16,208,128]{2,1,0:T(8,128)(2,1)S(1)} %bitcast.12, bf16[32,128,128]{2,1,0:T(8,128)(2,1)S(1)} %all-to-all-done.panel_ref, bf16[2,16,64,128]{3,2,1,0:T(8,128)(2,1)S(1)} %bitcast.13), custom_call_target="tpu_custom_call" | custom-call | flops 1610612736 | bytes 3145728 | tf_op jit(solution)/shard_map/second_product/pallas_call | solution.py:150
  114.3 22.3 %all_to_all.27 = bf16[16,64,128]{2,1,0:T(8,128)(2,1)S(1)} all-to-all(bf16[16,64,128]{2,1,0:T(8,128)(2,1)S(1)} %bitcast.14), channel_id=1, replica_groups=mesh['xh'=2,'y'=4,'core'=2,'z'=16,'xl'=2] {'z'}, dimensions={0} | all-to-all | bytes 524288 | tf_op jit(solution)/shard_map/all_to_all | solution.py:191
  136.7 0.7 select_add_fusion
  (5 shorter events, 0.1 us)
Async XLA Ops:
  0.9 6.1 %collective-permute-start = (bf16[8,128]{1,0:T(8,128)(2,1)S(1)}, bf16[8,128]{1,0:T(8,128)(2,1)S(1)}, u32[]{:S(2)}, u32[]{:S(2)}) collective-permute-start(bf16[8,128]{1,0:T(8,128)(2,1)S(1)} %broadcast_in_dim.14), channel_id=1, source_target_pairs={{0,1},{1,0},{2,3},{3,2},{4,5},{5,4},{6,7},{7,6},{8,9},{9,8},{10,11... | collective-permute-start | bytes 6152 | tf_op jit(solution)/shard_map/ppermute | solution.py:169
  4.3 0.8 copy-start
  5.1 0.7 copy-start.1
  7.1 45.3 %all-to-all-start = ((bf16[32,128,128]{2,1,0:T(8,128)(2,1)}), bf16[32,128,128]{2,1,0:T(8,128)(2,1)S(1)}, u32[]{:S(2)}, u32[]{:S(2)}) async-start(bf16[32,128,128]{2,1,0:T(8,128)(2,1)} %get-tuple-element.18), calls=%async_computation | async-start | bytes 2097152 | tf_op jit(solution)/shard_map/all_to_all | solution.py:173
  54.4 41.9 %copy-start.2 = (s32[64]{0:T(128)S(1)}, s32[64]{0:T(128)}, u32[]{:S(2)}) copy-start(s32[64]{0:T(128)} %param.6) | copy-start | bytes 772
  77.1 19.1 %all-to-all-start.2 = ((bf16[32,64,128]{2,1,0:T(8,128)(2,1)}), bf16[32,64,128]{2,1,0:T(8,128)(2,1)S(1)}, u32[]{:S(2)}, u32[]{:S(2)}) async-start(bf16[32,64,128]{2,1,0:T(8,128)(2,1)} %bitcast.4), calls=%async_computation.2 | async-start | bytes 1048576 | tf_op jit(solution)/shard_map/all_to_all | solution.py:184

commit v8 on v7

--- a/solution.py
+++ b/solution.py
@@ -75,7 +75,7 @@
     for j in range(4):
         right = rows_of(column_ref, j)
         row = slice(4 * (j // 2), 4 * (j // 2) + 1)
-        sums = jnp.zeros((1, 4 * N), F32)
+        sums = jnp.zeros((8, 4 * N), F32)
         for i in range(8):
             weights = weigh(rows_of(panel_ref, i), right)
             for k in range(2):
@@ -84,7 +84,8 @@
                 tile = jnp.exp2(weights[2 * N * k : 2 * N * (k + 1)] + offset).astype(BF)
                 top = 4 * N * i + 2 * N * k
                 kernel_ref[top : top + 2 * N, 4 * N * j : 4 * N * (j + 1)] = tile
-                sums = sums + jnp.sum(tile.astype(F32), axis=0, keepdims=True)
+                sums = sums + jnp.sum(tile.astype(F32).reshape(N // 4, 8, 4 * N), axis=0)
+        sums = jnp.sum(sums, axis=0, keepdims=True)
         sums_ref[2 * j : 2 * j + 1, :] = sums[:, :LANES]
         sums_ref[2 * j + 1 : 2 * j + 2, :] = sums[:, LANES:]
 
@@ -103,46 +104,51 @@
     )(half, column, panel)
 
 
-def first_kernel(parts_ref, column_ref, kernel_ref, out_ref, inv_ref):
-    inv = 1.0 / jnp.sqrt(jnp.sum(parts_ref[...], axis=0))
-    inv_ref[...] = inv
-    turned = inv.T
+def first_kernel(z_ref, parts_ref, column_ref, kernel_ref, out_ref, own_ref):
+    turned = (1.0 / jnp.sqrt(jnp.sum(parts_ref[...], axis=0))).T
+    z = z_ref[0]
+    own = jnp.zeros((N, LANES), F32)
     scaled = []
     for k in range(8):
+        inv = jnp.broadcast_to(turned[:, k : k + 1], (2 * N, LANES))
+        own = jnp.where(z == 2 * k, inv[:N], jnp.where(z == 2 * k + 1, inv[N:], own))
         prior = column_ref[2 * k : 2 * k + 2, 2 * N : 3 * N, :].reshape(2 * N, LANES).astype(F32)
-        scaled.append((turned[:, k : k + 1] * prior).astype(BF))
+        scaled.append((inv * prior).astype(BF))
+    own_ref[...] = own
     scaled = jnp.concatenate(scaled, 0)
     out_ref[...] = jnp.dot(kernel_ref[...], scaled, preferred_element_type=F32).astype(BF)
 
 
-def first_product(parts, column, kernel):
+def first_product(z, parts, column, kernel):
+    vmem = pl.BlockSpec(memory_space=pltpu.VMEM)
     return pl.pallas_call(
         first_kernel,
+        in_specs=[pl.BlockSpec(memory_space=pltpu.SMEM), vmem, vmem, vmem],
         out_shape=(
             jax.ShapeDtypeStruct((B, LANES), BF),
-            jax.ShapeDtypeStruct((8, LANES), F32),
+            jax.ShapeDtypeStruct((N, LANES), F32),
         ),
         compiler_params=PARAMS,
         cost_estimate=pl.CostEstimate(
             flops=2 * A * B * LANES, bytes_accessed=5 << 20, transcendentals=0
         ),
         name="first_product",
-    )(parts, column, kernel)
-
-
-def second_kernel(half_ref, column_ref, panel_ref, scaled_ref, out_ref):
+    )(z, parts, column, kernel)
+
+
+def second_kernel(half_ref, column_ref, panel_ref, scaled_ref, out_ref, stripe_ref):
     offsets = mask_offsets(half_ref, column_ref)
-    for i in range(4):
-        row = slice(4 * (i // 2), 4 * (i // 2) + 1)
-        left = rows_of(column_ref, i)
-        total = jnp.zeros((4 * N, LANES), F32)
+    scaled = scaled_ref[...].reshape(B, LANES)
+    for a in range(2):
+        row = slice(4 * a, 4 * a + 1)
         for j in range(8):
+            right = rows_of(panel_ref, j)
             offset = jnp.concatenate([offsets[2 * j][row], offsets[2 * j + 1][row]], 1)
-            tile = jnp.exp2(weigh(left, rows_of(panel_ref, j)) + offset).astype(BF)
-            at = 4 * j % 16
-            scaled = scaled_ref[j // 4, at : at + 4].reshape(4 * N, LANES)
-            total = total + jnp.dot(tile, scaled, preferred_element_type=F32)
-        out_ref[4 * N * i : 4 * N * (i + 1)] = total.astype(BF)
+            for i in range(2):
+                tile = jnp.exp2(weigh(rows_of(column_ref, 2 * a + i), right) + offset).astype(BF)
+                stripe_ref[a, 4 * N * i : 4 * N * (i + 1), 4 * N * j : 4 * N * (j + 1)] = tile
+        part = jnp.dot(stripe_ref[a], scaled, preferred_element_type=F32)
+        out_ref[8 * N * a : 8 * N * (a + 1)] = part.astype(BF)
 
 
 def second_product(half, column, panel, scaled):
@@ -151,6 +157,7 @@
         second_kernel,
         in_specs=[pl.BlockSpec(memory_space=pltpu.SMEM), vmem, vmem, vmem],
         out_shape=jax.ShapeDtypeStruct((A, LANES), BF),
+        scratch_shapes=[pltpu.VMEM((2, A // 2, B), BF)],
         compiler_params=PARAMS,
         cost_estimate=pl.CostEstimate(
             flops=2 * A * B * (256 + LANES), bytes_accessed=3 << 20, transcendentals=A * B
@@ -176,8 +183,7 @@
 
     block, sums = first_block(half, column, panel)
     parts = spread_gather(sums, "z", 16)
-    part, inv = first_product(parts, column, block)
-    inv_own = lax.dynamic_index_in_dim(inv.reshape(16, N), z, 0, False)[:, None]
+    part, inv_own = first_product(z.astype(jnp.int32).reshape(1), parts, column, block)
     classes_iota = jnp.arange(LANES, dtype=jnp.int32)
     seeds = SEED_WEIGHT * (seed_labels[:, None] == classes_iota[None, :]).astype(F32)
 

time: 138 us -> 136 us (0.986)
  blocking collectives: 95.6 us -> 115 us
  waiting for transfers between devices: 11.5 us -> 0.01 us
  starting transfers between devices: 18 us -> 10.4 us
  Pallas kernels: 8.7 us -> 7.15 us
    all_to_all x0 -> x1, blocking collectives: none -> 18.9 us  [per_device(): part = lax.all_to_all(part.reshape(32, N, LANES), PLANE, 0, 0, tiled=True)]
    all_to_all x1 -> x0, waiting for transfers between devices: 11.5 us -> none  [per_device(): part = lax.all_to_all(part.reshape(32, N, LANES), PLANE, 0, 0, tiled=True)]
    all_to_all x1 -> x0, starting transfers between devices: 7.59 us -> none  [per_device(): part = lax.all_to_all(part.reshape(32, N, LANES), PLANE, 0, 0, tiled=True)]
  transfers between devices with their start and end apart: 3 -> 2, of which waited for: 1 -> 0; matrix products, arithmetic and copies ran while one was open for 0% -> 0% of each run, Pallas kernels for 1% -> 1%
where the time goes in v8:
time: 136 us
  blocking collectives  115 us (85%)
  starting transfers between devices  10.4 us (8%)
  Pallas kernels  7.15 us (5%)
  local copies, waits for them, and re-layouts  1.76 us (1%)
  other arithmetic  1.63 us (1%)
    all_gather x1, blocking collectives, per_device(): column = lax.all_gather(jnp.concatenate([stacked] + flags, 0), 'z', axis=0)  38.2 us
    all_to_all x2, blocking collectives, spread_gather(): return lax.all_to_all(copies, axes, 0, 0, tiled=True)  32.9 us
    all_to_all x1, blocking collectives, per_device(): part = lax.all_to_all(part.reshape(16, N, LANES), 'z', 0, 0, tiled=True)  22.3 us
    all_to_all x1, blocking collectives, per_device(): part = lax.all_to_all(part.reshape(32, N, LANES), PLANE, 0, 0, tiled=True)  18.9 us
    all_to_all x1, starting transfers between devices, per_device(): panel = lax.all_to_all(loads, PLANE, 0, 0, tiled=True)  7.03 us
    ppermute x1, starting transfers between devices, per_device(): other = lax.ppermute(flags, 'xl', [(0, 1), (1, 0)])  3.39 us
  transfers between devices with their start and end apart: 2, of which 0 were waited for; matrix products, arithmetic and copies ran while one was open for 0% of the time, Pallas kernels for 1%

profile of v8, /device:TPU:32, one launch (start us, length us, event | category | flops | bytes accessed | tf_op | source)
XLA Modules:
  0.0 135.6 jit_solution(1134404458813940913)
XLA Ops:
  0.0 0.7 convert_bitcast_fusion
  0.7 0.1 broadcast_in_dim.10
  0.7 0.1 broadcast_in_dim.11
  0.8 0.1 broadcast_in_dim.12
  0.9 3.4 %collective-permute-start = (bf16[8,128]{1,0:T(8,128)(2,1)S(1)}, bf16[8,128]{1,0:T(8,128)(2,1)S(1)}, u32[]{:S(2)}, u32[]{:S(2)}) collective-permute-start(bf16[8,128]{1,0:T(8,128)(2,1)S(1)} %broadcast_in_dim.12), channel_id=1, source_target_pairs={{0,1},{1,0},{2,3},{3,2},{4,5},{5,4},{6,7},{7,6},{8,9},{9,8},{10,11... | collective-permute-start | bytes 6152 | tf_op jit(solution)/shard_map/ppermute | solution.py:176
  4.3 0.0 copy-start
  4.3 0.7 copy-done
  5.1 0.0 copy-start.1
  5.1 0.7 copy-done.1
  5.8 1.2 make_loads.1
  7.0 0.0 collective-permute-done
  7.0 0.1 broadcast_select_fusion
  7.1 7.0 %all-to-all-start = ((bf16[32,128,128]{2,1,0:T(8,128)(2,1)}), bf16[32,128,128]{2,1,0:T(8,128)(2,1)S(1)}, u32[]{:S(2)}, u32[]{:S(2)}) async-start(bf16[32,128,128]{2,1,0:T(8,128)(2,1)} %get-tuple-element.18), calls=%async_computation | async-start | bytes 2097152 | tf_op jit(solution)/shard_map/all_to_all | solution.py:180
  14.1 38.2 %all-gather = bf16[3328,128]{1,0:T(8,128)(2,1)S(1)} all-gather(bf16[208,128]{1,0:T(8,128)(2,1)S(1)} %pad_maximum_fusion), channel_id=2, replica_groups=mesh['xh'=2,'y'=4,'core'=2,'z'=16,'xl'=2] {'z'}, dimensions={0}, use_global_device_ids=true | all-gather | bytes 905216 | tf_op jit(solution)/shard_map/all_gather | solution.py:182
  52.3 0.0 all-to-all-done.panel_ref
  52.4 1.9 %first_block.1 = (bf16[2048,1024]{1,0:T(8,128)(2,1)S(1)}, f32[8,128]{1,0:T(8,128)S(1)}) custom-call(s32[1]{0:T(128)} %bitcast.1.half_ref, bf16[16,208,128]{2,1,0:T(8,128)(2,1)S(1)} %bitcast.8, bf16[32,128,128]{2,1,0:T(8,128)(2,1)S(1)} %all-to-all-done.panel_ref), custom_call_target="tpu_custom_call" | custom-call | flops 1073741824 | bytes 4194304 | tf_op jit(solution)/shard_map/first_block/pallas_call | solution.py:95
  54.2 0.0 copy-start.2
  54.3 20.4 %all_to_all.25.parts_ref = f32[16,8,128]{2,1,0:T(8,128)S(1)} all-to-all(f32[16,8,128]{2,1,0:T(8,128)S(1)} %broadcast_in_dim.13), channel_id=1, replica_groups=mesh['xh'=2,'y'=4,'core'=2,'z'=16,'xl'=2] {'z'}, dimensions={0} | all-to-all | bytes 131072 | tf_op jit(solution)/shard_map/all_to_all | solution.py:30
  74.6 1.5 %first_product.1 = (bf16[2048,128]{1,0:T(8,128)(2,1)S(1)}, f32[64,128]{1,0:T(8,128)S(1)}) custom-call(s32[1]{0:T(128)} %bitcast.z_ref, f32[16,8,128]{2,1,0:T(8,128)S(1)} %all_to_all.25.parts_ref, bf16[16,208,128]{2,1,0:T(8,128)(2,1)S(1)} %bitcast.9, bf16[2048,1024]{1,0:T(8,128)(2,1)S(1)} %get-tuple-element.20.kernel_ref), custom_call_target="tpu_custom_call" | custom-call | flops 536870912 | bytes 5242880 | tf_op jit(solution)/shard_map/first_product/pallas_call | solution.py:124
  76.1 18.9 %all_to_all.26 = bf16[32,64,128]{2,1,0:T(8,128)(2,1)S(1)} all-to-all(bf16[32,64,128]{2,1,0:T(8,128)(2,1)S(1)} %bitcast.12), channel_id=1, replica_groups=mesh['xh'=2,'y'=4,'core'=2,'z'=16,'xl'=2] {'core','xh','y','xl'}, dimensions={0} | all-to-all | bytes 1048576 | tf_op jit(solution)/shard_map/all_to_all | solution.py:190
  95.1 0.1 convert_reduce_fusion
  95.2 0.0 copy-done.2
  95.2 0.1 fusion.1
  95.3 12.6 %all_to_all.27 = bf16[16,64,128]{2,1,0:T(8,128)(2,1)S(1)} all-to-all(bf16[16,64,128]{2,1,0:T(8,128)(2,1)S(1)} %broadcast_in_dim.28), channel_id=1, replica_groups=mesh['xh'=2,'y'=4,'core'=2,'z'=16,'xl'=2] {'xh','y','xl'}, dimensions={0} | all-to-all | bytes 524288 | tf_op jit(solution)/shard_map/all_to_all | solution.py:30
  107.9 2.2 %all-gather.1 = bf16[32,64,128]{2,1,0:T(8,128)(2,1)S(1)} all-gather(bf16[16,64,128]{2,1,0:T(8,128)(2,1)S(1)} %all_to_all.27), channel_id=3, replica_groups=mesh['xh'=2,'y'=4,'core'=2,'z'=16,'xl'=2] {'core'}, dimensions={0}, use_global_device_ids=true | all-gather | bytes 786432 | tf_op jit(solution)/shard_map/all_gather | solution.py:195
  110.0 2.5 %second_product.1 = bf16[1024,128]{1,0:T(8,128)(2,1)S(1)} custom-call(s32[1]{0:T(128)} %bitcast.1.half_ref, bf16[16,208,128]{2,1,0:T(8,128)(2,1)S(1)} %bitcast.10, bf16[32,128,128]{2,1,0:T(8,128)(2,1)S(1)} %all-to-all-done.panel_ref, bf16[2,16,64,128]{3,2,1,0:T(8,128)(2,1)S(1)} %bitcast.11), custom_call_target="tpu_custom_call" | custom-call | flops 1610612736 | bytes 3145728 | tf_op jit(solution)/shard_map/second_product/pallas_call | solution.py:156
  112.6 22.3 %all_to_all.28 = bf16[16,64,128]{2,1,0:T(8,128)(2,1)S(1)} all-to-all(bf16[16,64,128]{2,1,0:T(8,128)(2,1)S(1)} %bitcast.13), channel_id=1, replica_groups=mesh['xh'=2,'y'=4,'core'=2,'z'=16,'xl'=2] {'z'}, dimensions={0} | all-to-all | bytes 524288 | tf_op jit(solution)/shard_map/all_to_all | solution.py:197
  134.9 0.7 select_add_fusion
  (4 shorter events, 0.1 us)
Async XLA Ops:
  0.9 6.1 %collective-permute-start = (bf16[8,128]{1,0:T(8,128)(2,1)S(1)}, bf16[8,128]{1,0:T(8,128)(2,1)S(1)}, u32[]{:S(2)}, u32[]{:S(2)}) collective-permute-start(bf16[8,128]{1,0:T(8,128)(2,1)S(1)} %broadcast_in_dim.12), channel_id=1, source_target_pairs={{0,1},{1,0},{2,3},{3,2},{4,5},{5,4},{6,7},{7,6},{8,9},{9,8},{10,11... | collective-permute-start | bytes 6152 | tf_op jit(solution)/shard_map/ppermute | solution.py:176
  4.3 0.8 copy-start
  5.1 0.7 copy-start.1
  7.1 45.3 %all-to-all-start = ((bf16[32,128,128]{2,1,0:T(8,128)(2,1)}), bf16[32,128,128]{2,1,0:T(8,128)(2,1)S(1)}, u32[]{:S(2)}, u32[]{:S(2)}) async-start(bf16[32,128,128]{2,1,0:T(8,128)(2,1)} %get-tuple-element.18), calls=%async_computation | async-start | bytes 2097152 | tf_op jit(solution)/shard_map/all_to_all | solution.py:180
  54.2 40.9 %copy-start.2 = (s32[64]{0:T(128)S(1)}, s32[64]{0:T(128)}, u32[]{:S(2)}) copy-start(s32[64]{0:T(128)} %param.6) | copy-start | bytes 772
